TPU v7x, 32 devices: a whole 2x2x4 slice. The times are simulated.
32 devices in a mesh: grp: 2 (over x), ens: 4 (over y, core), dp: 4 (over z).
Axes of the slice: x: 2, y: 2, z: 4, core: 2. Of those that a mesh axis runs over, the one named last changes fastest.
Arguments:
- states: float32 [16384, 34], P('dp'), may hold values from -6 to 6
- actions: float32 [16384, 6], P('dp'), may hold values from -0.95 to 0.95
- rewards: float32 [16384], P('dp'), may hold values from -6 to 6
- done: int32 [16384], P('dp'), may hold values 0 or 1
- noise: float32 [16384, 12], P('dp'), may hold values from -5 to 5
- counts: int32 [4], P('dp'), may hold values from 1 to 4096, as said below
- crit_edge: float32 [2, 8, 24, 256], P('grp', 'ens'), may hold values from -0.75 to 0.75
- crit_hidden: float32 [2, 8, 2, 256, 256], P('grp', 'ens'), may hold values from -0.375 to 0.375
- crit_bias: float32 [2, 8, 4, 256], P('grp', 'ens'), may hold values from -1 to 1
- edge_m: float32 [8, 24, 256], P('ens'), may hold values from -0.03125 to 0.03125
- edge_v: float32 [8, 24, 256], P('ens'), may hold values from 6.1035156e-05 to 0.00024414062
- hidden_m: float32 [8, 2, 256, 256], P('ens'), may hold values from -0.0046875 to 0.0046875
- hidden_v: float32 [8, 2, 256, 256], P('ens'), may hold values from 1.3732911e-06 to 5.4931643e-06
- bias_m: float32 [8, 4, 256], P('ens'), may hold values from -0.0125 to 0.0125
- bias_v: float32 [8, 4, 256], P('ens'), may hold values from 9.765625e-06 to 3.90625e-05
- act_edge: float32 [29, 256], replicated, may hold values from -0.75 to 0.75
- act_hidden: float32 [2, 256, 256], replicated, may hold values from -0.375 to 0.375
- act_bias: float32 [4, 256], replicated, may hold values from -1 to 1
- act_edge_m: float32 [29, 256], replicated, may hold values from -0.003125 to 0.003125
- act_edge_v: float32 [29, 256], replicated, may hold values from 6.1035155e-07 to 2.4414062e-06
- act_hidden_m: float32 [2, 256, 256], replicated, may hold values from -0.003125 to 0.003125
- act_hidden_v: float32 [2, 256, 256], replicated, may hold values from 6.1035155e-07 to 2.4414062e-06
- act_bias_m: float32 [4, 256], replicated, may hold values from -0.003125 to 0.003125
- act_bias_v: float32 [4, 256], replicated, may hold values from 6.1035155e-07 to 2.4414062e-06
Outputs:
- new_crit_edge: float32 [2, 8, 24, 256], P('grp', 'ens')
- new_crit_hidden: float32 [2, 8, 2, 256, 256], P('grp', 'ens')
- new_crit_bias: float32 [2, 8, 4, 256], P('grp', 'ens')
- new_edge_m: float32 [8, 24, 256], P('ens')
- new_edge_v: float32 [8, 24, 256], P('ens')
- new_hidden_m: float32 [8, 2, 256, 256], P('ens')
- new_hidden_v: float32 [8, 2, 256, 256], P('ens')
- new_bias_m: float32 [8, 4, 256], P('ens')
- new_bias_v: float32 [8, 4, 256], P('ens')
- new_act_edge: float32 [29, 256], replicated
- new_act_hidden: float32 [2, 256, 256], replicated
- new_act_bias: float32 [4, 256], replicated
- new_act_edge_m: float32 [29, 256], replicated
- new_act_edge_v: float32 [29, 256], replicated
- new_act_hidden_m: float32 [2, 256, 256], replicated
- new_act_hidden_v: float32 [2, 256, 256], replicated
- new_act_bias_m: float32 [4, 256], replicated
- new_act_bias_v: float32 [4, 256], replicated
- member_sums: float32 [8, 2], P('ens')
- actor_sums: float32 [2], replicated
Inputs may be any that keep to these rules, and one draw needn't show every extreme that they name: The counts rise along the shards, and the last shard's count is 4096.
All inputs are finite; a program needn't handle non-finite values. No bound on the sum of `done` on one device may be relied on, other than what follows from the above.
Results may differ from a plain program's by a relative error of at most 0.0003.
Values may be sent and summed in bfloat16 or wider, within the bound.
A program may use at most 704 MiB of HBM per device.

v0:
```python
import functools

import jax
import jax.numpy as jnp
from jax import lax
from jax.experimental import pallas as pl
from jax.experimental.pallas import tpu as pltpu
from jax.sharding import PartitionSpec as P

OBS = 17
ACT = 6
HID = 256
STEP = 5
FOLD_ROWS = 2816
LANES = 128

GAMMA = 0.99
ALPHA = 0.2
ETA = 1.0
LEARN = 0.03
BETA_ONE = 0.5
BETA_TWO = 0.5
DECAY = 0.01
EPS = 1e-08
TAU = 0.05
HALF_LOG_TWO_PI = 0.9189385332046727
LOG_TWO = 0.6931471805599453

F32 = jnp.float32
BF16 = jnp.bfloat16

CRITIC_SMALL, ACTOR_SMALL = 32, 64


def dot(a, b):
    return lax.dot_general(a, b, (((1,), (0,)), ((), ())), preferred_element_type=F32)


def dot_t(a, b):
    return lax.dot_general(a, b, (((1,), (1,)), ((), ())), preferred_element_type=F32)


def split(w):
    high = w.astype(BF16).astype(F32)
    return high, w - high


def halves(p):
    n = p.shape[0] // 2
    return p[:n] + p[n:]


def prep_input(stage, w1, edge, bias, n_in):
    stage[...] = jnp.zeros_like(stage)
    stage[0:OBS, :] = edge[0:OBS, :]
    stage[OBS : OBS + 1, :] = bias[0:1, :]
    if n_in > OBS:
        stage[24 : 24 + ACT, :] = edge[OBS : OBS + ACT, :]
    high, low = split(0.5 * stage[0:32, :])
    w1[...] = jnp.concatenate([high, low, high], 0).T.astype(BF16)


def prep_hidden(fwd, bwd, hidden):
    w = 0.5 * hidden
    if fwd is not None:
        high, low = split(w.T)
        fwd[...] = jnp.concatenate([high, low], 0).astype(BF16)
    if bwd is not None:
        high, low = split(w)
        bwd[...] = jnp.concatenate([high, low], 0).astype(BF16)


def silu_half(u):
    t = jnp.tanh(u)
    return u + u * t, t


def up(n, by):
    return -(-n // by) * by


def kernel(
    n_dp,
    rows,
    block,
    fold,
    states, actions, noise, rewards, done, counts, mask, c_edge, c_hidden, c_bias, a_edge, a_hidden, a_bias,
    out_c, out_a, out_small, out_high, out_rest, out_low,
    xs, ns, eps_s, far_x, far_e, here_x, here_e, x_b, pi_act, stage, vec, tvec, avec,
    small_out, small_in, high_out, high_in, rest_out, rest_in, low_out, low_in,
    w1, f0, f1, b0, b1, ga, t1w, eq,
    tw1, tf0, tf1, teq,
    aw1, af0, af1, ab0, ab1, ao, aot,
    h1x, h2x, h3s, s1, s2, s3, k1, k2, k3, d1s, d2s, d3s,
    heads, ah1x, ah2x, ah3, as1, as2, as3,
    value, unit_f, u_mine, u_peer, u_pair, u_far, u_total, dg_b, dv_b, dvh, row_sums,
    q_mine, q_peer, q_pair, q_far, q_total, q_own, least, far_least, least_in,
    acc_h1, acc_h1t, acc_h0, acc_h0t, acc_x, acc_t, acc_last, acc_o, acc_c1, acc_c0, acc_cx,
    part_c, part_a, sum_c, sum_a, in_h1, in_h0, in_sm, in_ac,
    fold_s, fold_r, sem_far_s, sem_far_r, sem_param_s, sem_param_r, sem_pi_s, sem_pi_r, sem_least_s, sem_least_r, es_s, es_r,
    rs_s, rs_r, ag_s, ag_r, xf_s, xf_r, ef_s, ef_r, sem_out, *boxes,
):
    g = lax.axis_index("grp")
    e = lax.axis_index("ens")
    z = lax.axis_index("dp")
    me = g * 4 + e
    blocks = rows // block
    extra = states.shape[1] - rows
    lower = z < n_dp // 2
    upper = z >= n_dp - n_dp // 2
    half = rows // 2
    online = g == 1
    targetd = g == 0
    critics = 8
    coded = bool(boxes)

    def dev(gg, ee):
        return {"grp": gg, "ens": ee}

    def remote(src, dst, send, recv, where):
        return pltpu.make_async_remote_copy(
            src_ref=src, dst_ref=dst, send_sem=send, recv_sem=recv, device_id=where, device_id_type=pl.DeviceIdType.MESH
        )

    barrier = pltpu.get_barrier_semaphore()
    for k in range(1, 8):
        p = lax.rem(me + k, 8)
        pl.semaphore_signal(barrier, inc=1, device_id=dev(p // 4, lax.rem(p, 4)), device_id_type=pl.DeviceIdType.MESH)
    for k in range(1, n_dp):
        pl.semaphore_signal(barrier, inc=1, device_id={"dp": lax.rem(z + k, n_dp)}, device_id_type=pl.DeviceIdType.MESH)

    def all_here():
        pl.semaphore_wait(barrier, 7 + n_dp - 1)

    def param_copy(what):
        src, dst = ((small_out, small_in), (high_out, high_in), (rest_out, rest_in), (low_out, low_in))[what]
        return remote(src, dst, sem_param_s.at[what], sem_param_r.at[what], dev(0, e))

    @pl.when(online)
    def _():
        small_out[...] = jnp.zeros_like(small_out)
        for k in range(2):
            small_out[32 * k : 32 * k + 24, :] = c_edge[1 - k]
            small_out[32 * k + 24 : 32 * k + 28, :] = c_bias[1 - k]
            high, low = split(c_hidden[1, k])
            high_out[k * HID : (k + 1) * HID, :] = high.astype(BF16)
            rest_out[k * HID : (k + 1) * HID, :] = low.astype(BF16)
            low_out[k * HID : (k + 1) * HID, :] = c_hidden[0, k].astype(BF16)
        all_here()
        for what in range(2):
            param_copy(what).start()

    lane_id = lax.broadcasted_iota(jnp.int32, (1, states.shape[1]), 1)
    if fold:
        code = jnp.where(lane_id < counts[0], 2.0, 0.0) + done[...].astype(F32)
    else:
        code = 2.0 * mask[...] + done[...].astype(F32)

    ones_row = jnp.ones((1, states.shape[1]), F32)
    xs[...] = jnp.zeros_like(xs)
    xs[0:OBS, :] = states[0:OBS, :]
    xs[OBS : OBS + 1, :] = ones_row
    xs[24 : 24 + ACT, :] = actions[...]
    eps_s[6:7, :] = rewards[...]
    eps_s[7:8, :] = code

    @pl.when(online)
    def _():
        eps_s[0:ACT, :] = noise[0:ACT, :]

    @pl.when(targetd)
    def _():
        eps_s[0:ACT, :] = noise[ACT : 2 * ACT, :]
        ns[...] = jnp.zeros_like(ns)
        ns[0:OBS, :] = states[OBS : 2 * OBS, :]
        ns[OBS : OBS + 1, :] = ones_row

    core = lax.rem(e, 2)
    other_core = e + 1 - 2 * core
    far_chip = lax.rem(e + 2, 4)

    def fold_copy(what, hop):
        here, there = ((here_e, far_e), (here_x, far_x))[what]
        if hop == 0:
            return remote(here.at[core], there.at[core], fold_s.at[what, 0], fold_r.at[what, 0], {"dp": n_dp - 1 - z})
        return remote(there.at[core], there.at[core], fold_s.at[what, 1], fold_r.at[what, 1], dev(g, other_core))

    def least_copy():
        return remote(least.at[:, rows:], far_least, sem_far_s, sem_far_r, {"dp": n_dp - 1 - z})

    def merge(into, blocks_of):
        first = rows - extra
        there = jnp.concatenate([blocks_of(b) for b in range(extra // LANES - 1, -1, -1)], 1).astype(F32)
        lanes = lax.broadcasted_iota(jnp.int32, (1, extra), 1) + first
        bound = (jnp.minimum(counts[0], rows) + LANES - 1) // LANES * LANES
        into[:, first:rows] = jnp.where(lanes < bound, into[:, first:rows], there)

    def in_halves(pieces):
        per = extra // LANES // 2
        return lambda b: pieces[b // per, :, (b % per) * LANES : (b % per + 1) * LANES]

    def fold_out():
        if fold:
            @pl.when(upper)
            def _():
                for h in range(2):
                    part = slice(rows + h * extra // 2, rows + (h + 1) * extra // 2)
                    here_e[h] = eps_s[:, part]
                    here_x[h] = xs[:, part].astype(BF16)
                for what in range(2):
                    fold_copy(what, 0).start()

    def fold_in():
        if fold:
            @pl.when(lower)
            def _():
                for what in range(2):
                    fold_copy(what, 0).wait_recv()
                    fold_copy(what, 1).start()
                for what in range(2):
                    fold_copy(what, 1).wait_recv()
                merge(eps_s, in_halves(far_e))
                merge(xs, in_halves(far_x))

    def put_x():
        high, low = split(xs[:, 0:rows])
        xin = high.astype(BF16)
        x_b[0:32, :] = xin
        x_b[32:64, :] = xin
        x_b[64:96, :] = low.astype(BF16)

    def prep_small(edge, bias, w1_, vec_, eq_, ga_, t1_):
        prep_input(stage, w1_, edge, bias, OBS + ACT)
        stage[...] = jnp.zeros_like(stage)
        stage[0:1, :] = 0.5 * bias[1:2, :]
        stage[1:2, :] = 0.5 * bias[2:3, :]
        stage[2:3, :] = edge[23:24, :]
        vec_[...] = stage[...].T
        vec_[0:1, 8:9] = bias[3:4, 0:1]
        stage[...] = jnp.zeros_like(stage)
        high, low = split(edge[23:24, :])
        stage[0:1, :] = high
        stage[1:2, :] = low
        eq_[...] = stage[0:16, :].astype(BF16)
        if ga_ is not None:
            stage[...] = jnp.zeros_like(stage)
            stage[0:ACT, :] = 0.5 * edge[OBS : OBS + ACT, :]
            high, low = split(stage[0:8, :])
            both = jnp.concatenate([high, low], 0)
            ga_[...] = both.astype(BF16)
            stage[0:16, :] = both
            t1_[...] = stage[...].T[:, 0:16].astype(BF16)

    def prep_actor():
        prep_input(stage, aw1, a_edge, a_bias, OBS)
        prep_hidden(af0, ab0, a_hidden[0])
        prep_hidden(af1, ab1, a_hidden[1])
        stage[...] = jnp.zeros_like(stage)
        stage[0:1, :] = 0.5 * a_bias[1:2, :]
        stage[1:2, :] = 0.5 * a_bias[2:3, :]
        stage[2:3, :] = a_bias[3:4, :]
        avec[...] = stage[...].T
        stage[...] = jnp.zeros_like(stage)
        stage[0:ACT, :] = a_edge[OBS : OBS + ACT, :]
        stage[8 : 8 + ACT, :] = a_edge[OBS + ACT : OBS + 2 * ACT, :]
        high, low = split(stage[0:16, :])
        ao[...] = jnp.concatenate([high, low], 0).astype(BF16)
        stage[...] = jnp.zeros_like(stage)
        stage[0 : 2 * ACT, :] = a_edge[OBS : OBS + 2 * ACT, :]
        high, low = split(stage[0:16, :])
        stage[0:32, :] = jnp.concatenate([high, low], 0)
        aot[...] = stage[...].T[:, 0:32].astype(BF16)

    prep_actor()

    def actor_layers(src):
        kept = []
        hb = None
        for w, b in ((aw1, None), (af0, 0), (af1, 1)):
            u = dot(w[...], src) if b is None else halves(dot(w[...], hb)) + avec[:, b : b + 1]
            h, t = silu_half(u)
            hb = h.astype(BF16)
            kept.append((hb, h, t))
        return kept

    ok8 = (lax.broadcasted_iota(jnp.int32, (8, 1), 0) < ACT).astype(F32)

    def actor_heads(hb, sl):
        out = halves(dot(ao[...], hb))
        eps = eps_s[:, sl]
        center = out[0:8] + avec[0:8, 2:3] * ok8
        th = jnp.tanh(out[8:16] + avec[6:14, 2:3] * ok8)
        log_std = 3.5 * th - 1.5
        spread_e = jnp.exp(log_std) * eps
        latent = center + spread_e
        soft = jnp.maximum(-2.0 * latent, 0.0) + jnp.log(1.0 + jnp.exp(-2.0 * jnp.abs(latent)))
        terms = -0.5 * eps * eps - log_std - HALF_LOG_TWO_PI - 2.0 * (LOG_TWO - latent - soft)
        logp = jnp.sum(terms * ok8, axis=0, keepdims=True)
        sample = jnp.tanh(latent) * ok8
        return sample, logp, th, spread_e

    put_x()

    @pl.when(online)
    def _():
        fold_out()
        prep_small(c_edge.at[0], c_bias.at[0], w1, vec, eq, ga, t1w)
        prep_hidden(f0, b0, c_hidden[0, 0])
        prep_hidden(f1, b1, c_hidden[0, 1])

    def least_online(k):
        return remote(least.at[:, 0:rows], least_in.at[k], sem_least_s.at[4 + k], sem_least_r.at[k], dev(1, lax.rem(e + k, 4)))

    def least_target(k):
        return remote(least.at[:, 0:rows], least_in.at[k], sem_least_s.at[k], sem_least_r.at[k], dev(0, lax.rem(e + k, 4)))

    def half_hidden(part, values):
        to = slice(part * HID, (part + 1) * HID)
        for k, (fwd, bwd) in enumerate(((f0, b0), (f1, b1))):
            w = 0.5 * values[k * HID : (k + 1) * HID, :].astype(F32)
            fwd[to, :] = w.T.astype(BF16)
            bwd[to, :] = w.astype(BF16)

    @pl.when(targetd)
    def _():
        for m in range(2):
            prep_small(c_edge.at[m], c_bias.at[m], tw1.at[m], tvec.at[m], teq.at[m], None, None)
            prep_hidden(tf0.at[m], None, c_hidden[m, 0])
            prep_hidden(tf1.at[m], None, c_hidden[m, 1])

        def body(i, _):
            @pl.when(i == 1)
            def _():
                all_here()
                fold_out()

            first = jnp.minimum(i * block, states.shape[1] - block)
            sl = pl.ds(pl.multiple_of(first, LANES), block)
            high, rest = split(ns[:, sl])
            nx, rest = high.astype(BF16), rest.astype(BF16)
            kept = actor_layers(jnp.concatenate([nx, nx, rest], 0))
            sample, logp, th, spread_e = actor_heads(kept[2][0], sl)
            high, rest = split(jnp.concatenate([ns[0:24, sl], sample], 0))
            nx = high.astype(BF16)
            nx = jnp.concatenate([nx, nx, rest.astype(BF16)], 0)
            low = None
            for m in range(2):
                h, t = silu_half(dot(tw1[m], nx))
                h, t = silu_half(halves(dot(tf0[m], h.astype(BF16))) + tvec[m, :, 0:1])
                h, t = silu_half(halves(dot(tf1[m], h.astype(BF16))) + tvec[m, :, 1:2])
                r = dot(teq[m], h.astype(BF16))
                q = r[0:1] + r[1:2] + tvec[m, 0:1, 8:9]
                low = q if low is None else jnp.minimum(low, q)
            least[:, sl] = low - ALPHA * logp
            return 0

        lax.fori_loop(0, blocks + (jnp.where(upper, 1, 0) if fold else 0), body, 0)
        if fold:
            @pl.when(upper)
            def _():
                least_copy().start()

        for what in range(2):
            param_copy(what).wait_recv()
        prep_small(small_in.at[0:24], small_in.at[24:32], w1, vec, eq, ga, t1w)
        half_hidden(0, high_in)

    def least_out():
        @pl.when(targetd)
        def _():
            if fold:
                @pl.when(lower)
                def _():
                    least_copy().wait_recv()
                    merge(least, lambda b: far_least[:, b * LANES : (b + 1) * LANES])

            for k in range(1, 4):
                least_target(k).start()
            for k in range(4):
                least_online(k).start()

    class EnsembleSum:
        def __init__(self, index, mine, peer, pair, far, total, only_online):
            self.index, self.mine, self.peer, self.pair, self.far, self.total, self.only_online = (
                index, mine, peer, pair, far, total, only_online,
            )

        def to_core(self):
            return remote(self.mine.at[1 - core], self.peer, es_s.at[self.index, 0], es_r.at[self.index, 0], dev(g, other_core))

        def to_chip(self, k):
            across = (1 - g, g, 1 - g)[k]
            where = dev(across, (e, far_chip, far_chip)[k])
            return remote(self.pair, self.far.at[k], es_s.at[self.index, 1 + k], es_r.at[self.index, 1 + k], where)

        def back(self):
            return remote(self.total.at[core], self.total.at[core], es_s.at[self.index, 4], es_r.at[self.index, 4], dev(g, other_core))

        def begin(self, first, second):
            self.mine[0] = first
            self.mine[1] = second
            self.to_core().start()

        def middle(self):
            self.to_core().wait_recv()
            self.pair[...] = self.mine[core] + self.peer[...]
            if not self.only_online:
                for k in range(3):
                    self.to_chip(k).start()
            else:
                @pl.when(targetd)
                def _():
                    self.to_chip(0).start()
                    self.to_chip(2).start()

                @pl.when(online)
                def _():
                    self.to_chip(1).start()

        def first_to_core(self, h, values):
            self.mine[h] = values

            @pl.when(core != h)
            def _():
                self.to_core().start()

            @pl.when(core == h)
            def _():
                self.middle()

        def last_of(self, h):
            @pl.when(core == h)
            def _():
                self.last()

        def back_of(self, h):
            @pl.when(core != h)
            def _():
                self.back().wait_recv()

        def last(self):
            for k in range(3):
                self.to_chip(k).wait_recv()
            self.total[core] = self.pair[...] + self.far[0] + self.far[1] + self.far[2]
            self.back().start()

        def whole(self):
            self.back().wait_recv()
            return jnp.concatenate([self.total[0], self.total[1]], 1)

        def sent(self):
            self.to_core().wait_send()
            if not self.only_online:
                for k in range(3):
                    self.to_chip(k).wait_send()
                self.back().wait_send()
            else:
                @pl.when(targetd)
                def _():
                    self.to_chip(0).wait_send()
                    self.to_chip(2).wait_send()

                @pl.when(online)
                def _():
                    self.to_chip(1).wait_send()
                    self.back().wait_send()

    unit_sum = EnsembleSum(0, u_mine, u_peer, u_pair, u_far, u_total, False)
    slope_sum = EnsembleSum(1, q_mine, q_peer, q_pair, q_far, q_total, True)

    def pi_copy(i):
        part = pi_act.at[:, pl.ds(pl.multiple_of(i * block, block), block)]
        return remote(part, part, sem_pi_s.at[i], sem_pi_r.at[i], dev(0, e))

    def body_p(i, _):
        sl = pl.ds(pl.multiple_of(i * block, block), block)

        @pl.when(i == 1)
        def _():
            fold_in()
            if fold:
                put_x()

        @pl.when(online)
        def _():
            kept = actor_layers(x_b[:, sl])
            if fold:
                for store, curve, (hb, h, t) in zip((ah1x, ah2x, ah3), (as1, as2, as3), kept):
                    store[0:HID, sl] = hb
                    curve[:, sl] = (1.0 + t) + h * (1.0 - t)
            sample, logp, th, spread_e = actor_heads(kept[2][0], sl)
            pi_act[:, sl] = sample
            heads[0:8, sl] = th
            heads[8:16, sl] = spread_e
            heads[16:17, sl] = logp
            pi_copy(i).start()

        @pl.when(jnp.logical_and(online, i == 0))
        def _():
            param_copy(2).start()

        @pl.when(targetd)
        def _():
            pi_copy(i).wait_recv()

        def act(u):
            h, t = silu_half(u)
            hb, tb = h.astype(BF16), t.astype(BF16)
            one = jnp.ones((), BF16)
            return hb, (one + tb) + hb * (one - tb)

        pin = jnp.concatenate([xs[0:24, sl], pi_act[:, sl]], 0).astype(BF16)
        h, a1 = act(dot(w1[:, 0:64], jnp.concatenate([pin, pin], 0)))
        h, a2 = act(dot(f0[0:HID, :], h) + vec[:, 0:1])
        h, a3 = act(dot(f1[0:HID, :], h) + vec[:, 1:2])
        r = dot(eq[...], h)
        q_own[:, sl] = r[0:1] + r[1:2] + vec[0:1, 8:9]
        d = vec[:, 2:3].astype(BF16) * a3
        d = dot(b1[0:HID, :], d).astype(BF16) * a2
        d = dot(b0[0:HID, :], d).astype(BF16) * a1
        unit_f[16:24, sl] = halves(dot(ga[...], d))
        return 0

    lax.fori_loop(0, blocks, body_p, 0)
    rid = lax.broadcasted_iota(jnp.int32, (8, 1), 0)
    packed = unit_f[16:24, :] + jnp.where(rid == 6, q_own[...], 0.0)
    slope_sum.begin(packed[:, 0:half], packed[:, half:rows])

    ones = (lax.broadcasted_iota(jnp.int32, (16, rows), 0) == 0).astype(BF16)
    h1x[HID : HID + 16, :] = ones
    h2x[HID : HID + 16, :] = ones

    def curves(u):
        h, t = silu_half(u)
        c = 1.0 + t
        d = 1.0 - t
        return h, c + h * d, (c * d) * (1.0 - u * t)

    @pl.when(targetd)
    def _():
        param_copy(2).wait_recv()
        half_hidden(1, rest_in)

    valid = jnp.where(eps_s[7:8, 0:rows] > 1.5, 1.0, 0.0)

    def body_a(i, _):
        @pl.when(i == 1)
        def _():
            slope_sum.middle()
            if fold:
                unit_sum.first_to_core(0, unit_f[0:8, 0:half])
            least_out()

            @pl.when(online)
            def _():
                param_copy(3).start()


        sl = pl.ds(pl.multiple_of(i * block, block), block)
        h, a1, q1 = curves(dot(w1[...], x_b[:, sl]))
        hb = h.astype(BF16)
        h1x[0:HID, sl] = hb
        s1[:, sl] = a1.astype(BF16)
        h, a2, q2 = curves(halves(dot(f0[...], hb)) + vec[:, 0:1])
        hb = h.astype(BF16)
        h2x[0:HID, sl] = hb
        s2[:, sl] = a2.astype(BF16)
        h, a3, q3 = curves(halves(dot(f1[...], hb)) + vec[:, 1:2])
        hb = h.astype(BF16)
        h3s[:, sl] = hb
        s3[:, sl] = a3.astype(BF16)
        r = dot(eq[...], hb)
        value[:, sl] = r[0:1] + r[1:2] + vec[0:1, 8:9]
        last = vec[:, 2:3]
        db = (last * a3).astype(BF16)
        d3s[:, sl] = db
        k3[:, sl] = (last * q3).astype(BF16)
        m = halves(dot(b1[...], db))
        db = (m * a2).astype(BF16)
        d2s[:, sl] = db
        k2[:, sl] = (m * q2).astype(BF16)
        m = halves(dot(b0[...], db))
        db = (m * a1).astype(BF16)
        d1s[:, sl] = db
        k1[:, sl] = (m * q1).astype(BF16)
        slope = halves(dot(ga[...], db))
        inv = lax.rsqrt(jnp.sum(slope * slope, axis=0, keepdims=True) + 0.01)
        unit_f[0:8, sl] = slope * inv
        unit_f[8:9, sl] = inv
        return 0

    lax.fori_loop(0, blocks, body_a, 0)
    if fold:
        unit_sum.first_to_core(1, unit_f[0:8, half:rows])
        unit_sum.last_of(0)
    else:
        unit_sum.begin(unit_f[0:8, 0:half], unit_f[0:8, half:rows])
        unit_sum.middle()

    class Exchange:
        def __init__(self, index, part, into, inbox, base, count, wide):
            self.index, self.part, self.into, self.inbox, self.base, self.count, self.wide = index, part, into, inbox, base, count, wide
            self.each = count // (n_dp * (4 if wide else 1))

        def rows_of(self, shard):
            first = self.base + (e * n_dp + shard if self.wide else shard) * self.each
            return pl.ds(pl.multiple_of(first, 8), self.each)

        def scatter(self, k):
            to = lax.rem(z + k, n_dp)
            return remote(
                self.part.at[self.rows_of(to)], self.inbox.at[k - 1], rs_s.at[self.index, k - 1, 0], rs_r.at[self.index, k - 1, 0], {"dp": to}
            )

        def gather(self, k):
            mine = self.into.at[self.rows_of(z)]
            return remote(mine, mine, ag_s.at[self.index, k - 1, 0], ag_r.at[self.index, k - 1, 0], {"dp": lax.rem(z + k, n_dp)})

        def across(self, k):
            there = self.into.at[self.rows_of(lax.rem(z + n_dp - k, n_dp))]
            return remote(there, there, xf_s.at[self.index, k, 0], xf_r.at[self.index, k, 0], dev(1 - g, e))

        def start(self):
            for k in range(1, n_dp):
                self.scatter(k).start()

        def reduce(self, along=True):
            total = self.part[self.rows_of(z), :]
            for k in range(1, n_dp):
                self.scatter(k).wait_recv()
                total = total + self.inbox[k - 1]
            self.into[self.rows_of(z), :] = total
            if along:
                for k in range(1, n_dp):
                    self.gather(k).start()
            self.across(0).start()

        def forward(self):
            for k in range(1, n_dp):
                self.gather(k).wait_recv()
                self.across(k).start()

        def sent(self):
            for k in range(1, n_dp):
                self.scatter(k).wait_send()
                self.gather(k).wait_send()
            for k in range(n_dp):
                self.across(k).wait_send()

        def arrived(self):
            for k in range(n_dp):
                self.across(k).wait_recv()

        def detour(self):
            self.across(0).wait_recv()
            for k in range(1, n_dp):
                self.gather(k).start()

        def back(self):
            for k in range(1, n_dp):
                self.across(k).wait_recv()

        def sent_detour(self):
            @pl.when(online)
            def _():
                for k in range(1, n_dp):
                    self.scatter(k).wait_send()
                self.across(0).wait_send()

            @pl.when(targetd)
            def _():
                for k in range(1, n_dp):
                    self.gather(k).wait_send()
                    self.across(k).wait_send()

    class Coded(Exchange):
        def __init__(self, index, part, out, base, count, lead, wide, boxes):
            self.index, self.part, self.out, self.base, self.count, self.lead, self.wide = index, part, out, base, count, lead, wide
            self.out_w, self.out_s, self.in_w, self.in_s, self.all_w, self.all_s = boxes
            self.each = count // (n_dp * (4 if wide else 1))

        def pack(self, x):
            top = jnp.maximum(jnp.max(jnp.abs(x), axis=0, keepdims=True), 1e-30)
            q = jnp.round(x * (32767.0 / top)).astype(jnp.int32)
            h = self.each // 2
            return jnp.bitwise_or(jnp.bitwise_and(q[:h], 65535), jnp.left_shift(q[h:], 16)), top * (1.0 / 32767.0)

        def unpack(self, w, scale):
            low = jnp.right_shift(jnp.left_shift(w, 16), 16)
            high = jnp.right_shift(w, 16)
            return jnp.concatenate([low, high], 0).astype(F32) * scale

        def scatter(self, k):
            to = lax.rem(z + k, n_dp)
            return Both([
                remote(o.at[to], i.at[k - 1], rs_s.at[self.index, k - 1, q], rs_r.at[self.index, k - 1, q], {"dp": to})
                for q, (o, i) in enumerate(((self.out_w, self.in_w), (self.out_s, self.in_s)))
            ])

        def gather(self, k):
            return Both([
                remote(
                    a.at[self.lead, z], a.at[self.lead, z], ag_s.at[self.index, k - 1, q], ag_r.at[self.index, k - 1, q],
                    {"dp": lax.rem(z + k, n_dp)},
                )
                for q, a in enumerate((self.all_w, self.all_s))
            ])

        def across(self, k):
            there = lax.rem(z + n_dp - k, n_dp)
            return Both([
                remote(
                    a.at[self.lead, there], a.at[self.lead, there], xf_s.at[self.index, k, q], xf_r.at[self.index, k, q], dev(1 - g, e)
                )
                for q, a in enumerate((self.all_w, self.all_s))
            ])

        def start(self):
            for shard in range(n_dp):
                w, scale = self.pack(self.part[self.rows_of(shard), :])
                self.out_w[shard] = w
                self.out_s[shard] = scale
            for k in range(1, n_dp):
                self.scatter(k).start()

        def reduce(self, along=True):
            total = self.part[self.rows_of(z), :]
            for k in range(1, n_dp):
                self.scatter(k).wait_recv()
                total = total + self.unpack(self.in_w[k - 1], self.in_s[k - 1])
            w, scale = self.pack(total)
            self.all_w[self.lead, z] = w
            self.all_s[self.lead, z] = scale
            if along:
                for k in range(1, n_dp):
                    self.gather(k).start()
            self.across(0).start()

        def decode(self):
            for lead in range(self.all_w.shape[0]):
                for shard in range(n_dp):
                    x = self.unpack(self.all_w[lead, shard], self.all_s[lead, shard])
                    if self.wide:
                        first = (lead * n_dp + shard) * self.each
                        self.out[first : first + self.each, :] = x
                    else:
                        first = self.base + shard * self.each
                        self.out[lead, first : first + self.each, :] = x

    class Both:
        def __init__(self, copies):
            self.copies = copies

        def start(self):
            for c in self.copies:
                c.start()

        def wait_recv(self):
            for c in self.copies:
                c.wait_recv()

        def wait_send(self):
            for c in self.copies:
                c.wait_send()

    if coded:
        box_h1, box_h0, box_ac = boxes[0:6], boxes[6:12], boxes[12:18]
    if coded:
        ex_h1 = Coded(0, part_c, sum_c, HID, HID, g, False, box_h1)
        ex_h0 = Coded(1, part_c, sum_c, 0, HID, g, False, box_h0)
        ex_ac = Coded(3, part_a, sum_a, 0, 2 * HID, e, True, box_ac)
        ex_as = Exchange(4, part_a, sum_a, in_ac, 2 * HID, ACTOR_SMALL, False)
        actor = (ex_ac, ex_as)
    else:
        ex_h1 = Exchange(0, part_c, sum_c.at[g], in_h1, HID, HID, False)
        ex_h0 = Exchange(1, part_c, sum_c.at[g], in_h0, 0, HID, False)
        ex_ac = Exchange(3, part_a, sum_a, in_ac, 0, part_a.shape[0], True)
        actor = (ex_ac,)
    ex_sm = Exchange(2, part_c, sum_c.at[g], in_sm, 2 * HID, part_c.shape[0] - 2 * HID, False)

    def spread_actor(k):
        if coded:
            mine = ex_ac.all_w.at[e]
        else:
            quarter = part_a.shape[0] // 4
            mine = sum_a.at[pl.ds(pl.multiple_of(e * quarter, 8), quarter)]
        return remote(mine, mine, ef_s.at[k - 1], ef_r.at[k - 1], dev(g, lax.rem(e + k, 4)))

    def spread_scale(k):
        mine = ex_ac.all_s.at[e]
        return remote(mine, mine, ef_s.at[2 + k], ef_r.at[2 + k], dev(g, lax.rem(e + k, 4)))

    def spread_start():
        for k in range(1, 4):
            spread_actor(k).start()
            if coded:
                spread_scale(k).start()

    lane = lax.broadcasted_iota(jnp.int32, (1, HID), 1)
    rid32 = lax.broadcasted_iota(jnp.int32, (32, 1), 0)

    def local(src, dst, k):
        return pltpu.make_async_copy(src, dst, sem_out.at[k])

    def own_outputs():
        return (
            local(small_out, out_small, 0), local(high_out, out_high, 1), local(rest_out, out_rest, 2), local(low_out, out_low, 5),
        )

    def far_outputs():
        return local(small_in, out_small, 0), local(high_in, out_high, 1), local(rest_in, out_rest, 2), local(low_in, out_low, 5)

    @pl.when(online)
    def _():
        slope_sum.last()
        total = slope_sum.whole() * (1.0 / critics)
        d_sample = -valid * total
        d_logp = ALPHA * valid
        sample = pi_act[...]
        th = heads[0:8, :]
        spread_e = heads[8:16, :]
        dz = (d_sample * (1.0 - sample * sample) + d_logp * 2.0 * sample) * ok8
        dls = (dz * spread_e - d_logp) * (3.5 * (1.0 - th * th)) * ok8
        heads[24:40, :] = jnp.zeros((16, rows), F32)
        heads[24:30, :] = dz[0:ACT]
        heads[30:36, :] = dls[0:ACT]
        actor_sum = jnp.sum(valid * (ALPHA * heads[16:17, :] - total[6:7]), axis=1, keepdims=True)
        done_rows = jnp.sum(valid, axis=1, keepdims=True)
        count = counts[0].astype(F32) if fold else 0.0
        for acc in (acc_c1, acc_c0, acc_cx, acc_o):
            acc[...] = jnp.zeros_like(acc)
        one16 = (lax.broadcasted_iota(jnp.int32, (16, block), 0) == 0).astype(BF16)
        if fold:
            ah1x[HID : HID + 16, :] = h1x[HID : HID + 16, :]
            ah2x[HID : HID + 16, :] = h1x[HID : HID + 16, :]

        def body_c(i, _):
            sl = pl.ds(pl.multiple_of(i * block, block), block)
            if fold:
                tall1, tall2, top = ah1x[:, sl], ah2x[:, sl], ah3[:, sl]
                slopes = [as1[:, sl], as2[:, sl], as3[:, sl]]
            else:
                kept = actor_layers(x_b[:, sl])
                tall1, tall2 = (jnp.concatenate([kept[k][0], one16], 0) for k in range(2))
                top = kept[2][0]
                slopes = [(1.0 + t) + h * (1.0 - t) for _, h, t in kept]
            do = heads[24:40, sl].astype(BF16)
            acc_o[0:16, :] += dot_t(do, top)
            d3 = (dot(aot[...], jnp.concatenate([do, do], 0)) * (0.5 * slopes[2])).astype(BF16)
            acc_c1[...] += dot_t(tall2, d3)
            d2 = (halves(dot(ab1[...], d3)) * slopes[1]).astype(BF16)
            acc_c0[...] += dot_t(tall1, d2)
            d1 = (halves(dot(ab0[...], d2)) * slopes[0]).astype(BF16)
            acc_cx[...] += dot_t(x_b[0:32, sl], d1)
            acc_o[16:32, 0:128] += dot_t(one16, jnp.concatenate([do, jnp.zeros((112, block), BF16)], 0))
            return 0

        lax.fori_loop(0, blocks, body_c, 0)
        part_a[0:HID, :] = acc_c0[0:HID, :]
        part_a[HID : 2 * HID, :] = acc_c1[0:HID, :]
        stats = jnp.where(lane == 0, actor_sum, jnp.where(lane == 1, count, jnp.where(lane == 2, done_rows, 0.0)))
        small = acc_cx[...]
        small = small + jnp.where(rid32 == 18, acc_c0[HID : HID + 1, :], 0.0)
        small = small + jnp.where(rid32 == 19, acc_c1[HID : HID + 1, :], 0.0)
        small = small + jnp.where(rid32 == 20, acc_o[16:17, :], 0.0)
        small = small + jnp.where(rid32 == 21, stats, 0.0)
        part_a[2 * HID : 2 * HID + 32, :] = small
        part_a[2 * HID + 32 : 2 * HID + 48, :] = acc_o[0:16, :]
        rest = part_a.shape[0] - 2 * HID - 48
        part_a[2 * HID + 48 :, :] = jnp.zeros((rest, HID), F32)
        for ex in actor:
            ex.start()

    @pl.when(targetd)
    def _():
        least_in[0] = least[:, 0:rows]
        for k in range(1, 4):
            least_target(k).wait_recv()

    @pl.when(online)
    def _():
        for k in range(4):
            least_online(k).wait_recv()

    rid16 = lax.broadcasted_iota(jnp.int32, (16, 1), 0)

    def directions(sl, spread):
        code = eps_s[7:8, sl]
        valid = jnp.where(code > 1.5, 1.0, 0.0)
        low = jnp.minimum(
            jnp.minimum(least_in[0, :, sl], least_in[1, :, sl]), jnp.minimum(least_in[2, :, sl], least_in[3, :, sl])
        )
        target = eps_s[6:7, sl] + GAMMA * (1.0 + 2.0 * valid - code) * low
        unit = unit_f[0:8, sl]
        inv = unit_f[8:9, sl]
        d_unit = (2.0 * ETA / (critics - 1)) * valid * (spread - unit)
        along = jnp.sum(d_unit * unit, axis=0, keepdims=True)
        dg = (d_unit - unit * along) * inv
        gap = value[:, sl] - target
        dv = 2.0 * valid * gap
        row_sums[0:1, sl] = valid * gap * gap
        row_sums[1:2, sl] = valid * jnp.sum(unit * (spread - unit), axis=0, keepdims=True)
        row_sums[2:3, sl] = dv
        dvh[:, sl] = 0.5 * dv
        dgb = dg.astype(BF16)
        dg_b[:, sl] = jnp.concatenate([dgb, dgb], 0)
        dv_b[:, sl] = jnp.where(rid16 == 0, dv, jnp.where(rid16 == 1, 1.0, 0.0)).astype(BF16)

    if not fold:
        unit_sum.last()
        directions(slice(0, rows), unit_sum.whole())

    for acc in (acc_h1, acc_h1t, acc_h0, acc_h0t, acc_x, acc_t, acc_last):
        acc[...] = jnp.zeros_like(acc)

    def body_b1(i, _):
        sl = pl.ds(pl.multiple_of(i * block, block), block)
        if fold:
            @pl.when(i == 0)
            def _():
                unit_sum.back_of(0)

            @pl.when(i == 1)
            def _():
                unit_sum.last_of(1)
                unit_sum.back_of(1)

            directions(sl, u_total[i])
        tp = dot(t1w[...], dg_b[:, sl])
        k1[:, sl] = (k1[:, sl].astype(F32) * tp).astype(BF16)
        th1 = (s1[:, sl].astype(F32) * tp).astype(BF16)
        tp = halves(dot(f0[...], th1))
        k2[:, sl] = (k2[:, sl].astype(F32) * tp).astype(BF16)
        th2 = (s2[:, sl].astype(F32) * tp).astype(BF16)
        tp = halves(dot(f1[...], th2))
        th3 = (s3[:, sl].astype(F32) * tp).astype(BF16)
        d3 = d3s[:, sl]
        ap3 = (dvh[:, sl] * d3.astype(F32) + k3[:, sl].astype(F32) * tp).astype(BF16)
        k3[:, sl] = ap3
        rows_dv = dv_b[:, sl]
        last = dot_t(rows_dv, h3s[:, sl])
        lone = dot_t(rows_dv, th3)
        acc_last[...] += last[0:8] + jnp.where(rid == 0, lone[1:2], 0.0)
        h3s[:, sl] = th1
        acc_h1[...] += dot_t(h2x[:, sl], ap3)
        acc_h1t[...] += dot_t(th2, d3)
        return 0

    def body_b2(i, _):
        sl = pl.ds(pl.multiple_of(i * block, block), block)
        ah = halves(dot(b1[...], k3[:, sl]))
        ap2 = (s2[:, sl].astype(F32) * ah + k2[:, sl].astype(F32)).astype(BF16)
        k2[:, sl] = ap2
        acc_h0[...] += dot_t(h1x[:, sl], ap2)
        acc_h0t[...] += dot_t(h3s[:, sl], d2s[:, sl])
        return 0

    def body_b3(i, _):
        sl = pl.ds(pl.multiple_of(i * block, block), block)
        ah = halves(dot(b0[...], k2[:, sl]))
        ap1 = (s1[:, sl].astype(F32) * ah + k1[:, sl].astype(F32)).astype(BF16)
        acc_x[...] += dot_t(x_b[0:32, sl], ap1)
        acc_t[...] += dot_t(dg_b[:, sl], d1s[:, sl])
        return 0

    lax.fori_loop(0, blocks, body_b1, 0)
    part_c[HID : 2 * HID, :] = acc_h1[0:HID, :] + 0.5 * acc_h1t[...]
    ex_h1.start()

    @pl.when(online)
    def _():
        for ex in actor:
            ex.reduce(False)

    lax.fori_loop(0, blocks, body_b2, 0)
    part_c[0:HID, :] = acc_h0[0:HID, :] + 0.5 * acc_h0t[...]
    ex_h0.start()
    ex_h1.reduce()

    @pl.when(targetd)
    def _():
        for ex in actor:
            ex.detour()

    lax.fori_loop(0, blocks, body_b3, 0)
    errors, diverse, dv_sum = (jnp.sum(row_sums[k : k + 1, :], axis=1, keepdims=True) for k in range(3))
    stats = jnp.where(lane == 0, errors, jnp.where(lane == 1, diverse, 0.0))
    small = acc_x[...]
    small = small + jnp.where(rid32 == 18, acc_h0[HID : HID + 1, :], 0.0)
    small = small + jnp.where(rid32 == 19, acc_h1[HID : HID + 1, :], 0.0)
    small = small + jnp.where(rid32 == 20, stats, 0.0)
    small = small + jnp.where(rid32 == 22, jnp.where(lane == 0, dv_sum, 0.0), 0.0)
    small = small + jnp.where(rid32 == 23, acc_last[0:1, :], 0.0)
    part_c[2 * HID : 2 * HID + 24, :] = small[0:24]
    part_c[2 * HID + 24 : 2 * HID + 32, :] = small[24:32] + 0.5 * acc_t[0:8, :]
    rest = part_c.shape[0] - 2 * HID - 32
    if rest:
        part_c[2 * HID + 32 :, :] = jnp.zeros((rest, HID), F32)
    ex_sm.start()
    ex_h1.forward()
    ex_h0.reduce()
    ex_sm.reduce()

    @pl.when(targetd)
    def _():
        for ex in actor:
            ex.forward()
        spread_start()

    ex_h0.forward()
    ex_sm.forward()

    @pl.when(online)
    def _():
        for ex in actor:
            ex.back()
        spread_start()


    @pl.when(online)
    def _():
        for copy in own_outputs():
            copy.start()

    @pl.when(targetd)
    def _():
        param_copy(3).wait_recv()
        for copy in far_outputs():
            copy.start()

    for k in range(1, 4):
        spread_actor(k).wait_recv()
        if coded:
            spread_scale(k).wait_recv()
    if coded:
        ex_ac.decode()
    copy_a = local(sum_a, out_a, 3)
    copy_a.start()
    for ex in (ex_h1, ex_h0, ex_sm):
        ex.arrived()
    if coded:
        ex_h1.decode()
        ex_h0.decode()
    copy_c = local(sum_c, out_c, 4)
    copy_c.start()

    @pl.when(online)
    def _():
        for what in range(4):
            param_copy(what).wait_send()

        def pi_sent(i, _):
            pi_copy(i).wait_send()
            return 0

        lax.fori_loop(0, blocks, pi_sent, 0)

    @pl.when(targetd)
    def _():
        for k in range(1, 4):
            least_target(k).wait_send()
        for k in range(4):
            least_online(k).wait_send()

    if fold:
        @pl.when(upper)
        def _():
            for what in range(2):
                fold_copy(what, 0).wait_send()

        @pl.when(lower)
        def _():
            for what in range(2):
                fold_copy(what, 1).wait_send()

        @pl.when(jnp.logical_and(upper, targetd))
        def _():
            least_copy().wait_send()

    unit_sum.sent()
    slope_sum.sent()
    for ex in actor:
        ex.sent_detour()
    for k in range(1, 4):
        spread_actor(k).wait_send()
        if coded:
            spread_scale(k).wait_send()
    for ex in (ex_h1, ex_h0, ex_sm):
        ex.sent()
    copy_a.wait()
    copy_c.wait()

    @pl.when(online)
    def _():
        for copy in own_outputs():
            copy.wait()

    @pl.when(targetd)
    def _():
        for copy in far_outputs():
            copy.wait()


def sizes(n_dp):
    return 2 * HID + up(CRITIC_SMALL, 8 * n_dp), up(2 * HID + ACTOR_SMALL, 32 * n_dp)


def fused(n_dp, rows, block, fold, data, own, aparams):
    v = pltpu.VMEM
    big = lambda n=HID: v((n, rows), BF16)
    dma = pltpu.SemaphoreType.DMA
    size_c, size_a = sizes(n_dp)
    coded = 2 * HID % (64 * n_dp) == 0
    h8 = lambda *n: v((*n, 8, rows // 2), F32)
    sums = [h8(2), h8(), h8(), h8(3), h8(2)]
    extra = (data[0].shape[1] - rows) // 2 if fold else LANES
    moved = [v((2, 32, extra), BF16), v((2, 8, extra), F32)]
    size = data[0].shape[1]
    kept = (lambda n, t: v((n, rows), t)) if fold else (lambda n, t: v((16, LANES), t))
    scratch = [
        v((32, size), F32), v((32, size), F32), v((8, size), F32), *moved, *moved,
        v((96, rows), BF16), v((8, rows), F32),
        v((128, HID), F32), v((HID, 128), F32), v((2, HID, 128), F32), v((HID, 128), F32),
        v((64, HID), F32), v((64, HID), F32), *[v((2 * HID, HID), BF16) for _ in range(6)],
        v((HID, 96), BF16), v((512, HID), BF16), v((512, HID), BF16), v((512, HID), BF16), v((512, HID), BF16),
        v((16, HID), BF16), v((HID, 16), BF16), v((16, HID), BF16),
        v((2, HID, 96), BF16), v((2, 512, HID), BF16), v((2, 512, HID), BF16), v((2, 16, HID), BF16),
        v((HID, 96), BF16), v((512, HID), BF16), v((512, HID), BF16), v((512, HID), BF16), v((512, HID), BF16),
        v((32, HID), BF16), v((HID, 32), BF16),
        big(272), big(272), big(), big(), big(), big(), big(), big(), big(), big(), big(), big(),
        v((40, rows), F32), kept(272, BF16), kept(272, BF16), kept(HID, BF16), kept(HID, F32), kept(HID, F32), kept(HID, F32),
        v((1, rows), F32), v((24, rows), F32), *sums,
        v((16, rows), BF16), v((16, rows), BF16), v((1, rows), F32), v((8, rows), F32),
        *sums, v((1, rows), F32),
        v((1, size), F32), v((1, 2 * extra), F32), v((4, 1, rows), F32),
        v((272, HID), F32), v((HID, HID), F32), v((272, HID), F32), v((HID, HID), F32),
        v((32, HID), F32), v((16, HID), F32), v((8, HID), F32), v((32, HID), F32),
        v((272, HID), F32), v((272, HID), F32), v((32, HID), F32),
        v((size_c, HID), F32), v((size_a, HID), F32), v((2, size_c, HID), F32), v((size_a, HID), F32),
        *[v((1, 8, HID) if coded else (n_dp - 1, HID // n_dp, HID), F32) for _ in range(2)],
        v((n_dp - 1, (size_c - 2 * HID) // n_dp, HID), F32),
        v((n_dp - 1, (ACTOR_SMALL if coded else size_a // 4) // n_dp, HID), F32),
        dma((2, 2)), dma((2, 2)), dma, dma, dma((4,)), dma((4,)), dma((rows // block,)), dma((rows // block,)), dma((8,)), dma((4,)), dma((2, 5)), dma((2, 5)),
        dma((5, n_dp - 1, 2)), dma((5, n_dp - 1, 2)), dma((5, n_dp - 1, 2)), dma((5, n_dp - 1, 2)), dma((5, n_dp, 2)), dma((5, n_dp, 2)),
        dma((6,)), dma((6,)), dma((6,)),
    ]
    if coded:
        for each, lead in ((HID // n_dp, 2), (HID // n_dp, 2), (2 * HID // (4 * n_dp), 4)):
            word, scale = (each // 2, HID), (1, HID)
            for outer in ((n_dp,), (n_dp - 1,), (lead, n_dp)):
                scratch += [v((*outer, *word), jnp.int32), v((*outer, *scale), F32)]
    spec = pl.BlockSpec(memory_space=pltpu.VMEM)
    anyspace = pl.BlockSpec(memory_space=pl.ANY)
    shape = lambda *s: jax.ShapeDtypeStruct(s, F32)
    return pl.pallas_call(
        functools.partial(kernel, n_dp, rows, block, fold),
        out_shape=(
            shape(2, size_c, HID), shape(size_a, HID), shape(64, HID), *[jax.ShapeDtypeStruct((2 * HID, HID), BF16)] * 3,
        ),
        in_specs=[spec] * 5 + [pl.BlockSpec(memory_space=pltpu.SMEM)] + [spec] * 7,
        out_specs=(anyspace,) * 6,
        scratch_shapes=scratch,
        compiler_params=pltpu.CompilerParams(collective_id=0 if fold else 1, has_side_effects=True, vmem_limit_bytes=63 * 2**20),
        name="edac_gradients" if fold else "edac_rest",
    )(*data, *own, *aparams)


def adamw(param, grad, first, second):
    first_new = BETA_ONE * first + (1.0 - BETA_ONE) * grad
    second_new = BETA_TWO * second + (1.0 - BETA_TWO) * grad * grad
    ratio = first_new / (1.0 - BETA_ONE**STEP) / (jnp.sqrt(second_new / (1.0 - BETA_TWO**STEP)) + EPS)
    return (param - LEARN * (ratio + DECAY * param), first_new, second_new)


def update_kernel(*refs):
    n_in, n_out = 24, 20
    src, dst = refs[:n_in], refs[n_in : n_in + n_out]
    rest = refs[n_in + n_out :]
    buf, res = rest[:n_in], rest[n_in : n_in + n_out]
    ge, gb, gae, gab, sem_in, sem_out = rest[n_in + n_out :]
    gc, ga, own_e, own_h, own_b, on_s, on_high, on_rest, low_h, em, ev, hm, hv, bm, bv, ae, ah, ab, aem, aev, ahm, ahv, abm, abv = buf
    o_e, o_h, o_b, o_em, o_ev, o_hm, o_hv, o_bm, o_bv, o_ae, o_ah, o_ab, o_aem, o_aev, o_ahm, o_ahv, o_abm, o_abv, o_ms, o_as = res
    online = lax.axis_index("grp") == 1
    index = {id(b): k for k, b in enumerate(buf)}
    out_index = {id(r): k for k, r in enumerate(res)}

    def read(b, slot=0, at=lambda r: r):
        k = index[id(b)]
        return pltpu.make_async_copy(at(src[k]), at(b), sem_in.at[k, slot])

    def write(r, slot=0, at=lambda x: x):
        k = out_index[id(r)]
        return pltpu.make_async_copy(at(r), at(dst[k]), sem_out.at[k, slot])

    def matrix(m, k):
        rows = slice(k * HID, (k + 1) * HID)
        par = [read(low_h, k, lambda r: r.at[rows])] if m == 0 else [
            read(on_high, k, lambda r: r.at[rows]), read(on_rest, k, lambda r: r.at[rows])
        ]
        mine = [read(b, 2 * m + k, lambda r: r.at[m, k]) for b in (own_h, hm, hv)]
        return [read(gc, 2 * m + k, lambda r: r.at[1 - m, rows])] + par + mine

    def actor_matrix(k):
        rows = slice(k * HID, (k + 1) * HID)
        return [read(ga, k, lambda r: r.at[rows])] + [read(b, k, lambda r: r.at[k]) for b in (ah, ahm, ahv)]

    stats = read(ga, 2, lambda r: r.at[2 * HID : 2 * HID + ACTOR_SMALL])
    small_reads = [read(gc, 4, lambda r: r.at[:, 2 * HID :]), stats] + [
        read(b) for b in (own_e, own_b, on_s, em, ev, bm, bv, ae, ab, aem, aev, abm, abv)
    ]
    order = [(0, 0), (0, 1), (1, 0), (1, 1)]
    stats.start()
    for copy in matrix(*order[0]):
        copy.start()
    for copy in small_reads:
        if copy is not stats:
            copy.start()
    for at in order[1:]:
        for copy in matrix(*at):
            copy.start()
    for k in range(2):
        for copy in actor_matrix(k):
            copy.start()

    gas = ga.at[2 * HID : 2 * HID + ACTOR_SMALL]
    stats.wait()
    scale = 1.0 / gas[21:22, 1:2]
    writes = []

    def put(copy):
        copy.start()
        writes.append(copy)

    def critic(own, param, grad, first, second):
        master, m_new, v_new = adamw(jnp.where(online, own, param), grad, first, second)
        polyak = TAU * master.astype(BF16).astype(F32) + (1.0 - TAU) * own
        return jnp.where(online, master, polyak), m_new, v_new

    def do_matrix(m, k):
        for copy in matrix(m, k):
            copy.wait()
        rows = slice(k * HID, (k + 1) * HID)
        param = low_h[rows, :].astype(F32) if m == 0 else on_high[rows, :].astype(F32) + on_rest[rows, :].astype(F32)
        o_h[m, k], o_hm[m, k], o_hv[m, k] = critic(own_h[m, k], param, gc[1 - m, rows, :] * scale, hm[m, k], hv[m, k])
        for r in (o_h, o_hm, o_hv):
            put(write(r, 2 * m + k, lambda x: x.at[m, k]))

    do_matrix(0, 0)
    for copy in small_reads:
        if copy is not stats:
            copy.wait()
    for m in range(2):
        small = gc.at[1 - m, 2 * HID : 2 * HID + 32]
        ge[0:OBS, :] = small[0:OBS, :]
        ge[OBS : OBS + ACT, :] = small[24 : 24 + ACT, :]
        ge[23:24, :] = small[23:24, :]
        gb[0:3, :] = small[17:20, :]
        gb[3:4, :] = small[22:23, :]
        first = 32 * (1 - m)
        o_e[m], o_em[m], o_ev[m] = critic(own_e[m], on_s[first : first + 24], ge[...] * scale, em[m], ev[m])
        o_b[m], o_bm[m], o_bv[m] = critic(own_b[m], on_s[first + 24 : first + 28], gb[...] * scale, bm[m], bv[m])
        o_ms[m : m + 1, :] = small[20:21, 0:2]
    gae[0:OBS, :] = gas[0:OBS, :]
    gae[OBS : OBS + 2 * ACT, :] = gas[32 : 32 + 2 * ACT, :]
    gab[0:3, :] = gas[17:20, :]
    gab[3:4, :] = gas[20:21, :]
    o_ae[...], o_aem[...], o_aev[...] = adamw(ae[...], gae[...] * scale, aem[...], aev[...])
    o_ab[...], o_abm[...], o_abv[...] = adamw(ab[...], gab[...] * scale, abm[...], abv[...])
    o_as[...] = gas[21:22, 0:2]
    for r in (o_e, o_b, o_em, o_ev, o_bm, o_bv, o_ae, o_ab, o_aem, o_aev, o_abm, o_abv, o_ms, o_as):
        put(write(r))
    for at in order[1:]:
        do_matrix(*at)
    for k in range(2):
        for copy in actor_matrix(k):
            copy.wait()
        grad = ga[k * HID : (k + 1) * HID, :] * scale
        o_ah[k], o_ahm[k], o_ahv[k] = adamw(ah[k], grad, ahm[k], ahv[k])
        for r in (o_ah, o_ahm, o_ahv):
            put(write(r, k, lambda x: x.at[k]))
    for copy in writes:
        copy.wait()


def update(grads, own, online, moments, aparams, amoments):
    shape = lambda *s: jax.ShapeDtypeStruct(s, F32)
    e_, h_, b_ = shape(2, 24, HID), shape(2, 2, HID, HID), shape(2, 4, HID)
    ae_, ah_, ab_ = shape(29, HID), shape(2, HID, HID), shape(4, HID)
    outs = (e_, h_, b_, e_, e_, h_, h_, b_, b_, ae_, ah_, ab_, ae_, ae_, ah_, ah_, ab_, ab_, shape(2, 2), shape(1, 2))
    args = (*grads, *own, *online, *moments, *aparams, *amoments)
    anyspace = pl.BlockSpec(memory_space=pl.ANY)
    room = [pltpu.VMEM(a.shape, a.dtype) for a in args]
    return pl.pallas_call(
        update_kernel,
        out_shape=outs,
        in_specs=[anyspace] * len(args),
        out_specs=(anyspace,) * len(outs),
        scratch_shapes=room
        + [pltpu.VMEM(o.shape, o.dtype) for o in outs]
        + [pltpu.VMEM((24, HID), F32), pltpu.VMEM((4, HID), F32), pltpu.VMEM((29, HID), F32), pltpu.VMEM((4, HID), F32)]
        + [pltpu.SemaphoreType.DMA((len(args), 5)), pltpu.SemaphoreType.DMA((len(outs), 4))],
        compiler_params=pltpu.CompilerParams(vmem_limit_bytes=40 * 2**20),
        name="adamw",
    )(*args)


def body(
    n_dp,
    states, actions, rewards, done, noise, counts,
    crit_edge, crit_hidden, crit_bias, edge_m, edge_v, hidden_m, hidden_v, bias_m, bias_v,
    act_edge, act_hidden, act_bias, act_edge_m, act_edge_v, act_hidden_m, act_hidden_v, act_bias_m, act_bias_v,
):
    size = states.shape[0]
    own = (crit_edge[0], crit_hidden[0], crit_bias[0])
    aparams = (act_edge, act_hidden, act_bias)
    data = (states.T, actions.T, noise.T, rewards[None], done[None], counts)
    moments = (edge_m, edge_v, hidden_m, hidden_v, bias_m, bias_v)
    amoments = (act_edge_m, act_edge_v, act_hidden_m, act_hidden_v, act_bias_m, act_bias_v)
    rows = FOLD_ROWS if size > FOLD_ROWS else size
    grad_c, grad_a, *online = fused(n_dp, rows, rows // 2, True, (*data, rewards[None]), own, aparams)

    def finish(grad_c, grad_a):
        return update((grad_c, grad_a), own, online, moments, aparams, amoments)

    def with_rest():
        z = lax.axis_index("dp")
        partner = lax.ppermute(counts, "dp", [(k, n_dp - 1 - k) for k in range(n_dp)])
        at = jnp.arange(size, dtype=jnp.int32)
        taken = (rows // LANES - 1 - (at - rows) // LANES) * LANES >= (jnp.minimum(partner, rows) + LANES - 1) // LANES * LANES
        taken = jnp.where(z >= n_dp - n_dp // 2, taken, False)
        left = jnp.logical_and(jnp.logical_and(at >= rows, at < counts), jnp.logical_not(taken))
        more_c, more_a, *_ = fused(n_dp, size, size // 16, False, (*data, left.astype(F32)[None]), own, aparams)
        return finish(grad_c + more_c, grad_a + more_a)

    sums = grad_a[2 * HID + 21]
    out = lax.cond(sums[1] != sums[2], with_rest, lambda: finish(grad_c, grad_a))
    return (*(o[None] for o in out[:3]), *out[3:19], out[19][0])


def solution(mesh):
    member = P("grp", "ens", None, None)
    hidden = P("grp", "ens", None, None, None)
    mom = P("ens", None, None)
    mom_h = P("ens", None, None, None)
    return jax.shard_map(
        functools.partial(body, mesh.shape["dp"]),
        mesh=mesh,
        in_specs=(
            P("dp", None), P("dp", None), P("dp"), P("dp"), P("dp", None), P("dp"),
            member, hidden, member, mom, mom, mom_h, mom_h, mom, mom,
        ) + (P(),) * 9,
        out_specs=(member, hidden, member, mom, mom, mom_h, mom_h, mom, mom) + (P(),) * 9 + (P("ens", None), P()),
        check_vma=False,
    )
```

profile of v0, /device:TPU:0, one launch (start us, length us, event | category | flops | bytes accessed | tf_op | source)
XLA Modules:
  0.0 81.1 jit_solution(18401010337133293465)
XLA Ops:
  1.3 0.0 copy-start.1
  1.3 0.0 copy-start.7
  1.3 0.0 copy-start.9
  1.3 0.0 copy-start.12
  1.3 0.0 copy-start.18
  1.4 0.0 copy-start.19
  1.4 70.0 %edac_gradients.1 = (f32[2,544,256]{2,1,0:T(8,128)}, f32[640,256]{1,0:T(8,128)}, f32[64,256]{1,0:T(8,128)S(1)}, bf16[512,256]{1,0:T(8,128)(2,1)}, bf16[512,256]{1,0:T(8,128)(2,1)}, /*index=5*/bf16[512,256]{1,0:T(8,128)(2,1)}) custom-call(f32[34,4096]{1,0:T(8,128)} %bitcast.22, f32[6,4096]{1,0:T(8,128)} %bitcast.29, f32[12,4096]{1,0:T(8,128)} %bitcast.24, ...), custom_call_target="tpu_custom_call" | custom-call | tf_op jit(solution)/shard_map/edac_gradients/pallas_call | solution.py:1155
  71.3 1.3 %fusion = (f32[1,1]{1,0:T(1,128)}, f32[1,1]{1,0:T(1,128)}) fusion(f32[640,256]{1,0:T(8,128)} %get-tuple-element.294), kind=kLoop, calls=%fused_computation.5 | loop fusion | bytes 16 | tf_op jit(solution)/shard_map/slice | solution.py:1336
  74.0 0.0 copy-done.1
  74.0 0.0 copy-done.7
  74.0 0.0 copy-done.9
  74.0 0.0 copy-done.12
  74.0 0.0 copy-done.18
  74.0 0.0 copy-done.19
  74.0 6.9 %conditional.1 = (f32[2,24,256]{2,1,0:T(8,128)}, f32[2,24,256]{2,1,0:T(8,128)}, f32[2,2,256,256]{3,2,1,0:T(8,128)}, f32[2,2,256,256]{3,2,1,0:T(8,128)}, f32[2,4,...) conditional(s32[]{:T(128)} %bitcast.18, ...), branch_computations={%region_0.0_spmd, %region_1.2_spmd} | conditional | flops 548885 | bytes 27362168 | solution.py:1336
  74.3 6.7 %adamw.2 = (f32[2,24,256]{2,1,0:T(8,128)}, f32[2,2,256,256]{3,2,1,0:T(8,128)}, f32[2,4,256]{2,1,0:T(4,128)}, f32[2,24,256]{2,1,0:T(8,128)}, f32[2,24,256]{2,1,0:...) custom-call(f32[2,544,256]{2,1,0:T(8,128)} %get-tuple-element.152.re, ...), custom_call_target="tpu_custom_call" | custom-call | tf_op jit(solution)/shard_map/cond/branch_0_fun/adamw/pallas_call | solution.py:1293
Async XLA Ops:
  1.3 72.7 %copy-start.1 = (f32[2,256,256]{2,1,0:T(8,128)S(1)}, f32[2,256,256]{2,1,0:T(8,128)}, u32[]{:S(2)}) copy-start(f32[2,256,256]{2,1,0:T(8,128)} %a_hidden.1) | copy-start | bytes 1572868
  1.3 72.7 %copy-start.7 = (f32[4096,12]{0,1:T(8,128)S(1)}, f32[4096,12]{0,1:T(8,128)}, u32[]{:S(2)}) copy-start(f32[4096,12]{0,1:T(8,128)} %param.30) | copy-start | bytes 589828
  1.3 72.7 %copy-start.9 = (f32[1,2,24,256]{3,2,1,0:T(8,128)S(1)}, f32[1,2,24,256]{3,2,1,0:T(8,128)}, u32[]{:S(2)}) copy-start(f32[1,2,24,256]{3,2,1,0:T(8,128)} %param.32) | copy-start | bytes 147460
  1.3 72.7 %copy-start.12 = (f32[29,256]{1,0:T(8,128)S(1)}, f32[29,256]{1,0:T(8,128)}, u32[]{:S(2)}) copy-start(f32[29,256]{1,0:T(8,128)} %a_edge.1) | copy-start | bytes 89092
  1.3 72.7 %copy-start.18 = (f32[4096]{0:T(1024)S(1)}, f32[4096]{0:T(1024)}, u32[]{:S(2)}) copy-start(f32[4096]{0:T(1024)} %param.28) | copy-start | bytes 49156
  1.4 72.7 %copy-start.19 = (f32[29,256]{1,0:T(8,128)S(1)}, f32[29,256]{1,0:T(8,128)}, u32[]{:S(2)}) copy-start(f32[29,256]{1,0:T(8,128)} %param.44) | copy-start | bytes 89092
where the time goes:
time: 81.4 us; the launch traced here: 81.1 us
  Pallas kernels  76.7 us (94%)
  between operations  2.89 us (4%)
  local copies, waits for them, and re-layouts  1.36 us (2%)
    pallas_call x1, Pallas kernels, fused(): pl.pallas_call(functools.partial(kernel, n_dp, rows, block, fold), out_sh...  70 us
    pallas_call x1, Pallas kernels, update(): pl.pallas_call(update_kernel, out_shape=outs, in_specs=[anyspace] * len(a...  6.69 us

commit v1 on v0

--- a/solution.py
+++ b/solution.py
@@ -88,16 +88,16 @@
     out_c, out_a, out_small, out_high, out_rest, out_low,
     xs, ns, eps_s, far_x, far_e, here_x, here_e, x_b, pi_act, stage, vec, tvec, avec,
     small_out, small_in, high_out, high_in, rest_out, rest_in, low_out, low_in,
-    w1, f0, f1, b0, b1, ga, t1w, eq,
+    w1, f0, f1, b0, b1, ga, t1w, eq, pw, pv, pq, pg, pf, pb,
     tw1, tf0, tf1, teq,
     aw1, af0, af1, ab0, ab1, ao, aot,
     h1x, h2x, h3s, s1, s2, s3, k1, k2, k3, d1s, d2s, d3s,
     heads, ah1x, ah2x, ah3, as1, as2, as3,
     value, unit_f, u_mine, u_peer, u_pair, u_far, u_total, dg_b, dv_b, dvh, row_sums,
-    q_mine, q_peer, q_pair, q_far, q_total, q_own, least, far_least, least_in,
+    q_mine, q_peer, q_pair, q_far, q_total, least, far_least, least_in,
     acc_h1, acc_h1t, acc_h0, acc_h0t, acc_x, acc_t, acc_last, acc_o, acc_c1, acc_c0, acc_cx,
     part_c, part_a, sum_c, sum_a, in_h1, in_h0, in_sm, in_ac,
-    fold_s, fold_r, sem_far_s, sem_far_r, sem_param_s, sem_param_r, sem_pi_s, sem_pi_r, sem_least_s, sem_least_r, es_s, es_r,
+    fold_s, fold_r, sem_far_s, sem_far_r, sem_param_s, sem_param_r, sem_least_s, sem_least_r, es_s, es_r,
     rs_s, rs_r, ag_s, ag_r, xf_s, xf_r, ef_s, ef_r, sem_out, *boxes,
 ):
     g = lax.axis_index("grp")
@@ -133,7 +133,13 @@
         pl.semaphore_wait(barrier, 7 + n_dp - 1)
 
     def param_copy(what):
-        src, dst = ((small_out, small_in), (high_out, high_in), (rest_out, rest_in), (low_out, low_in))[what]
+        src, dst = (
+            (small_out.at[0:32], small_in.at[0:32]),
+            (high_out, high_in),
+            (rest_out, rest_in),
+            (low_out, low_in),
+            (small_out.at[32:64], small_in.at[32:64]),
+        )[what]
         return remote(src, dst, sem_param_s.at[what], sem_param_r.at[what], dev(0, e))
 
     @pl.when(online)
@@ -147,7 +153,7 @@
             rest_out[k * HID : (k + 1) * HID, :] = low.astype(BF16)
             low_out[k * HID : (k + 1) * HID, :] = c_hidden[0, k].astype(BF16)
         all_here()
-        for what in range(2):
+        for what in range(3):
             param_copy(what).start()
 
     lane_id = lax.broadcasted_iota(jnp.int32, (1, states.shape[1]), 1)
@@ -249,7 +255,8 @@
             both = jnp.concatenate([high, low], 0)
             ga_[...] = both.astype(BF16)
             stage[0:16, :] = both
-            t1_[...] = stage[...].T[:, 0:16].astype(BF16)
+            if t1_ is not None:
+                t1_[...] = stage[...].T[:, 0:16].astype(BF16)
 
     def prep_actor():
         prep_input(stage, aw1, a_edge, a_bias, OBS)
@@ -307,6 +314,14 @@
         prep_small(c_edge.at[0], c_bias.at[0], w1, vec, eq, ga, t1w)
         prep_hidden(f0, b0, c_hidden[0, 0])
         prep_hidden(f1, b1, c_hidden[0, 1])
+        for k, (fwd, bwd) in enumerate(((f0, b0), (f1, b1))):
+            pf[0, k] = fwd[0:HID, :]
+            pb[0, k] = bwd[0:HID, :]
+            w = 0.5 * c_hidden[1, k]
+            pf[1, k] = w.T.astype(BF16)
+            pb[1, k] = w.astype(BF16)
+        pw[0], pv[0], pq[0], pg[0] = w1[...], vec[...], eq[...], ga[...]
+        prep_small(c_edge.at[1], c_bias.at[1], pw.at[1], pv.at[1], pq.at[1], pg.at[1], None)
 
     def least_online(k):
         return remote(least.at[:, 0:rows], least_in.at[k], sem_least_s.at[4 + k], sem_least_r.at[k], dev(1, lax.rem(e + k, 4)))
@@ -360,10 +375,14 @@
             def _():
                 least_copy().start()
 
-        for what in range(2):
+        fold_in()
+        if fold:
+            put_x()
+        for what in range(3):
             param_copy(what).wait_recv()
         prep_small(small_in.at[0:24], small_in.at[24:32], w1, vec, eq, ga, t1w)
         half_hidden(0, high_in)
+        half_hidden(1, rest_in)
 
     def least_out():
         @pl.when(targetd)
@@ -381,9 +400,8 @@
 
     class EnsembleSum:
         def __init__(self, index, mine, peer, pair, far, total, only_online):
-            self.index, self.mine, self.peer, self.pair, self.far, self.total, self.only_online = (
-                index, mine, peer, pair, far, total, only_online,
-            )
+            self.index, self.mine, self.peer, self.pair, self.far, self.total = index, mine, peer, pair, far, total
+            self.chips = (1,) if only_online else (0, 1, 2)
 
         def to_core(self):
             return remote(self.mine.at[1 - core], self.peer, es_s.at[self.index, 0], es_r.at[self.index, 0], dev(g, other_core))
@@ -404,18 +422,8 @@
         def middle(self):
             self.to_core().wait_recv()
             self.pair[...] = self.mine[core] + self.peer[...]
-            if not self.only_online:
-                for k in range(3):
-                    self.to_chip(k).start()
-            else:
-                @pl.when(targetd)
-                def _():
-                    self.to_chip(0).start()
-                    self.to_chip(2).start()
-
-                @pl.when(online)
-                def _():
-                    self.to_chip(1).start()
+            for k in self.chips:
+                self.to_chip(k).start()
 
         def first_to_core(self, h, values):
             self.mine[h] = values
@@ -439,9 +447,11 @@
                 self.back().wait_recv()
 
         def last(self):
-            for k in range(3):
+            total = self.pair[...]
+            for k in self.chips:
                 self.to_chip(k).wait_recv()
-            self.total[core] = self.pair[...] + self.far[0] + self.far[1] + self.far[2]
+                total = total + self.far[k]
+            self.total[core] = total
             self.back().start()
 
         def whole(self):
@@ -450,39 +460,26 @@
 
         def sent(self):
             self.to_core().wait_send()
-            if not self.only_online:
-                for k in range(3):
-                    self.to_chip(k).wait_send()
-                self.back().wait_send()
-            else:
-                @pl.when(targetd)
-                def _():
-                    self.to_chip(0).wait_send()
-                    self.to_chip(2).wait_send()
-
-                @pl.when(online)
-                def _():
-                    self.to_chip(1).wait_send()
-                    self.back().wait_send()
+            for k in self.chips:
+                self.to_chip(k).wait_send()
+            self.back().wait_send()
 
     unit_sum = EnsembleSum(0, u_mine, u_peer, u_pair, u_far, u_total, False)
     slope_sum = EnsembleSum(1, q_mine, q_peer, q_pair, q_far, q_total, True)
 
-    def pi_copy(i):
-        part = pi_act.at[:, pl.ds(pl.multiple_of(i * block, block), block)]
-        return remote(part, part, sem_pi_s.at[i], sem_pi_r.at[i], dev(0, e))
-
-    def body_p(i, _):
-        sl = pl.ds(pl.multiple_of(i * block, block), block)
-
-        @pl.when(i == 1)
-        def _():
-            fold_in()
-            if fold:
-                put_x()
-
-        @pl.when(online)
-        def _():
+    rid = lax.broadcasted_iota(jnp.int32, (8, 1), 0)
+
+    @pl.when(online)
+    def _():
+        def body_p(i, _):
+            sl = pl.ds(pl.multiple_of(i * block, block), block)
+
+            @pl.when(i == 1)
+            def _():
+                fold_in()
+                if fold:
+                    put_x()
+
             kept = actor_layers(x_b[:, sl])
             if fold:
                 for store, curve, (hb, h, t) in zip((ah1x, ah2x, ah3), (as1, as2, as3), kept):
@@ -493,38 +490,32 @@
             heads[0:8, sl] = th
             heads[8:16, sl] = spread_e
             heads[16:17, sl] = logp
-            pi_copy(i).start()
-
-        @pl.when(jnp.logical_and(online, i == 0))
-        def _():
-            param_copy(2).start()
-
-        @pl.when(targetd)
-        def _():
-            pi_copy(i).wait_recv()
-
-        def act(u):
-            h, t = silu_half(u)
-            hb, tb = h.astype(BF16), t.astype(BF16)
-            one = jnp.ones((), BF16)
-            return hb, (one + tb) + hb * (one - tb)
-
-        pin = jnp.concatenate([xs[0:24, sl], pi_act[:, sl]], 0).astype(BF16)
-        h, a1 = act(dot(w1[:, 0:64], jnp.concatenate([pin, pin], 0)))
-        h, a2 = act(dot(f0[0:HID, :], h) + vec[:, 0:1])
-        h, a3 = act(dot(f1[0:HID, :], h) + vec[:, 1:2])
-        r = dot(eq[...], h)
-        q_own[:, sl] = r[0:1] + r[1:2] + vec[0:1, 8:9]
-        d = vec[:, 2:3].astype(BF16) * a3
-        d = dot(b1[0:HID, :], d).astype(BF16) * a2
-        d = dot(b0[0:HID, :], d).astype(BF16) * a1
-        unit_f[16:24, sl] = halves(dot(ga[...], d))
-        return 0
-
-    lax.fori_loop(0, blocks, body_p, 0)
-    rid = lax.broadcasted_iota(jnp.int32, (8, 1), 0)
-    packed = unit_f[16:24, :] + jnp.where(rid == 6, q_own[...], 0.0)
-    slope_sum.begin(packed[:, 0:half], packed[:, half:rows])
+            pin = jnp.concatenate([xs[0:24, sl], sample], 0).astype(BF16)
+            unit_f[16:24, sl] = jnp.zeros((8, block), F32)
+
+            def member(m, _):
+                def act(u):
+                    h, t = silu_half(u)
+                    hb, tb = h.astype(BF16), t.astype(BF16)
+                    one = jnp.ones((), BF16)
+                    return hb, (one + tb) + hb * (one - tb)
+
+                h, a1 = act(dot(pw[m][:, 0:64], jnp.concatenate([pin, pin], 0)))
+                h, a2 = act(dot(pf[m, 0], h) + pv[m][:, 0:1])
+                h, a3 = act(dot(pf[m, 1], h) + pv[m][:, 1:2])
+                r = dot(pq[m], h)
+                q = r[0:1] + r[1:2] + pv[m][0:1, 8:9]
+                d = pv[m][:, 2:3].astype(BF16) * a3
+                d = dot(pb[m, 1], d).astype(BF16) * a2
+                d = dot(pb[m, 0], d).astype(BF16) * a1
+                unit_f[16:24, sl] += halves(dot(pg[m], d)) + jnp.where(rid == 6, q, 0.0)
+                return 0
+
+            lax.fori_loop(0, 2, member, 0)
+            return 0
+
+        lax.fori_loop(0, blocks, body_p, 0)
+        slope_sum.begin(unit_f[16:24, 0:half], unit_f[16:24, half:rows])
 
     ones = (lax.broadcasted_iota(jnp.int32, (16, rows), 0) == 0).astype(BF16)
     h1x[HID : HID + 16, :] = ones
@@ -536,17 +527,15 @@
         d = 1.0 - t
         return h, c + h * d, (c * d) * (1.0 - u * t)
 
-    @pl.when(targetd)
-    def _():
-        param_copy(2).wait_recv()
-        half_hidden(1, rest_in)
-
     valid = jnp.where(eps_s[7:8, 0:rows] > 1.5, 1.0, 0.0)
 
     def body_a(i, _):
         @pl.when(i == 1)
         def _():
-            slope_sum.middle()
+            @pl.when(online)
+            def _():
+                slope_sum.middle()
+
             if fold:
                 unit_sum.first_to_core(0, unit_f[0:8, 0:half])
             least_out()
@@ -554,6 +543,7 @@
             @pl.when(online)
             def _():
                 param_copy(3).start()
+                param_copy(4).start()
 
 
         sl = pl.ds(pl.multiple_of(i * block, block), block)
@@ -1025,6 +1015,7 @@
     @pl.when(targetd)
     def _():
         param_copy(3).wait_recv()
+        param_copy(4).wait_recv()
         for copy in far_outputs():
             copy.start()
 
@@ -1046,14 +1037,8 @@
 
     @pl.when(online)
     def _():
-        for what in range(4):
+        for what in range(5):
             param_copy(what).wait_send()
-
-        def pi_sent(i, _):
-            pi_copy(i).wait_send()
-            return 0
-
-        lax.fori_loop(0, blocks, pi_sent, 0)
 
     @pl.when(targetd)
     def _():
@@ -1078,7 +1063,11 @@
             least_copy().wait_send()
 
     unit_sum.sent()
-    slope_sum.sent()
+
+    @pl.when(online)
+    def _():
+        slope_sum.sent()
+
     for ex in actor:
         ex.sent_detour()
     for k in range(1, 4):
@@ -1124,6 +1113,8 @@
         v((64, HID), F32), v((64, HID), F32), *[v((2 * HID, HID), BF16) for _ in range(6)],
         v((HID, 96), BF16), v((512, HID), BF16), v((512, HID), BF16), v((512, HID), BF16), v((512, HID), BF16),
         v((16, HID), BF16), v((HID, 16), BF16), v((16, HID), BF16),
+        v((2, HID, 96), BF16), v((2, HID, 128), F32), v((2, 16, HID), BF16), v((2, 16, HID), BF16),
+        v((2, 2, HID, HID), BF16), v((2, 2, HID, HID), BF16),
         v((2, HID, 96), BF16), v((2, 512, HID), BF16), v((2, 512, HID), BF16), v((2, 16, HID), BF16),
         v((HID, 96), BF16), v((512, HID), BF16), v((512, HID), BF16), v((512, HID), BF16), v((512, HID), BF16),
         v((32, HID), BF16), v((HID, 32), BF16),
@@ -1131,7 +1122,7 @@
         v((40, rows), F32), kept(272, BF16), kept(272, BF16), kept(HID, BF16), kept(HID, F32), kept(HID, F32), kept(HID, F32),
         v((1, rows), F32), v((24, rows), F32), *sums,
         v((16, rows), BF16), v((16, rows), BF16), v((1, rows), F32), v((8, rows), F32),
-        *sums, v((1, rows), F32),
+        *sums,
         v((1, size), F32), v((1, 2 * extra), F32), v((4, 1, rows), F32),
         v((272, HID), F32), v((HID, HID), F32), v((272, HID), F32), v((HID, HID), F32),
         v((32, HID), F32), v((16, HID), F32), v((8, HID), F32), v((32, HID), F32),
@@ -1140,7 +1131,7 @@
         *[v((1, 8, HID) if coded else (n_dp - 1, HID // n_dp, HID), F32) for _ in range(2)],
         v((n_dp - 1, (size_c - 2 * HID) // n_dp, HID), F32),
         v((n_dp - 1, (ACTOR_SMALL if coded else size_a // 4) // n_dp, HID), F32),
-        dma((2, 2)), dma((2, 2)), dma, dma, dma((4,)), dma((4,)), dma((rows // block,)), dma((rows // block,)), dma((8,)), dma((4,)), dma((2, 5)), dma((2, 5)),
+        dma((2, 2)), dma((2, 2)), dma, dma, dma((5,)), dma((5,)), dma((8,)), dma((4,)), dma((2, 5)), dma((2, 5)),
         dma((5, n_dp - 1, 2)), dma((5, n_dp - 1, 2)), dma((5, n_dp - 1, 2)), dma((5, n_dp - 1, 2)), dma((5, n_dp, 2)), dma((5, n_dp, 2)),
         dma((6,)), dma((6,)), dma((6,)),
     ]

time: 81.4 us -> 74.1 us (0.910)
  Pallas kernels: 76.7 us -> 69.4 us
    pallas_call x1, Pallas kernels: 70 us -> 62.7 us  [fused(): pl.pallas_call(functools.partial(kernel, n_dp, rows, block, fold), out_sh...]
where the time goes in v1:
time: 74.1 us; the launch traced here: 73.9 us
  Pallas kernels  69.4 us (94%)
  between operations  2.89 us (4%)
  local copies, waits for them, and re-layouts  1.36 us (2%)
    pallas_call x1, Pallas kernels, fused(): pl.pallas_call(functools.partial(kernel, n_dp, rows, block, fold), out_sh...  62.7 us
    pallas_call x1, Pallas kernels, update(): pl.pallas_call(update_kernel, out_shape=outs, in_specs=[anyspace] * len(a...  6.69 us

profile of v1, /device:TPU:0, one launch (start us, length us, event | category | flops | bytes accessed | tf_op | source)
XLA Modules:
  0.0 73.9 jit_solution(9792840545990606997)
XLA Ops:
  1.3 0.0 copy-start.1
  1.3 0.0 copy-start.7
  1.3 0.0 copy-start.9
  1.3 0.0 copy-start.12
  1.3 0.0 copy-start.18
  1.4 0.0 copy-start.19
  1.4 62.7 %edac_gradients.1 = (f32[2,544,256]{2,1,0:T(8,128)}, f32[640,256]{1,0:T(8,128)}, f32[64,256]{1,0:T(8,128)S(1)}, bf16[512,256]{1,0:T(8,128)(2,1)}, bf16[512,256]{1,0:T(8,128)(2,1)}, /*index=5*/bf16[512,256]{1,0:T(8,128)(2,1)}) custom-call(f32[34,4096]{1,0:T(8,128)} %bitcast.22, f32[6,4096]{1,0:T(8,128)} %bitcast.29, f32[12,4096]{1,0:T(8,128)} %bitcast.24, ...), custom_call_target="tpu_custom_call" | custom-call | tf_op jit(solution)/shard_map/edac_gradients/pallas_call | solution.py:1146
  64.0 1.3 %fusion = (f32[1,1]{1,0:T(1,128)}, f32[1,1]{1,0:T(1,128)}) fusion(f32[640,256]{1,0:T(8,128)} %get-tuple-element.294), kind=kLoop, calls=%fused_computation.5 | loop fusion | bytes 16 | tf_op jit(solution)/shard_map/slice | solution.py:1327
  66.7 0.0 copy-done.1
  66.7 0.0 copy-done.7
  66.7 0.0 copy-done.9
  66.7 0.0 copy-done.12
  66.7 0.0 copy-done.18
  66.7 0.0 copy-done.19
  66.7 6.9 %conditional.1 = (f32[2,24,256]{2,1,0:T(8,128)}, f32[2,24,256]{2,1,0:T(8,128)}, f32[2,2,256,256]{3,2,1,0:T(8,128)}, f32[2,2,256,256]{3,2,1,0:T(8,128)}, f32[2,4,...) conditional(s32[]{:T(128)} %bitcast.18, ...), branch_computations={%region_0.0_spmd, %region_1.2_spmd} | conditional | flops 548885 | bytes 27362168 | solution.py:1327
  67.0 6.7 %adamw.2 = (f32[2,24,256]{2,1,0:T(8,128)}, f32[2,2,256,256]{3,2,1,0:T(8,128)}, f32[2,4,256]{2,1,0:T(4,128)}, f32[2,24,256]{2,1,0:T(8,128)}, f32[2,24,256]{2,1,0:...) custom-call(f32[2,544,256]{2,1,0:T(8,128)} %get-tuple-element.152.re, ...), custom_call_target="tpu_custom_call" | custom-call | tf_op jit(solution)/shard_map/cond/branch_0_fun/adamw/pallas_call | solution.py:1284
Async XLA Ops:
  1.3 65.4 %copy-start.1 = (f32[2,256,256]{2,1,0:T(8,128)S(1)}, f32[2,256,256]{2,1,0:T(8,128)}, u32[]{:S(2)}) copy-start(f32[2,256,256]{2,1,0:T(8,128)} %a_hidden.1) | copy-start | bytes 1572868
  1.3 65.4 %copy-start.7 = (f32[4096,12]{0,1:T(8,128)S(1)}, f32[4096,12]{0,1:T(8,128)}, u32[]{:S(2)}) copy-start(f32[4096,12]{0,1:T(8,128)} %param.30) | copy-start | bytes 589828
  1.3 65.4 %copy-start.9 = (f32[1,2,24,256]{3,2,1,0:T(8,128)S(1)}, f32[1,2,24,256]{3,2,1,0:T(8,128)}, u32[]{:S(2)}) copy-start(f32[1,2,24,256]{3,2,1,0:T(8,128)} %param.32) | copy-start | bytes 147460
  1.3 65.4 %copy-start.12 = (f32[29,256]{1,0:T(8,128)S(1)}, f32[29,256]{1,0:T(8,128)}, u32[]{:S(2)}) copy-start(f32[29,256]{1,0:T(8,128)} %a_edge.1) | copy-start | bytes 89092
  1.3 65.4 %copy-start.18 = (f32[4096]{0:T(1024)S(1)}, f32[4096]{0:T(1024)}, u32[]{:S(2)}) copy-start(f32[4096]{0:T(1024)} %param.28) | copy-start | bytes 49156
  1.4 65.4 %copy-start.19 = (f32[29,256]{1,0:T(8,128)S(1)}, f32[29,256]{1,0:T(8,128)}, u32[]{:S(2)}) copy-start(f32[29,256]{1,0:T(8,128)} %param.44) | copy-start | bytes 89092

commit v2 on v1

--- a/solution.py
+++ b/solution.py
@@ -29,7 +29,7 @@
 F32 = jnp.float32
 BF16 = jnp.bfloat16
 
-CRITIC_SMALL, ACTOR_SMALL = 32, 64
+CRITIC_SMALL, ACTOR_SMALL = 32, 32
 
 
 def dot(a, b):
@@ -95,7 +95,7 @@
     heads, ah1x, ah2x, ah3, as1, as2, as3,
     value, unit_f, u_mine, u_peer, u_pair, u_far, u_total, dg_b, dv_b, dvh, row_sums,
     q_mine, q_peer, q_pair, q_far, q_total, least, far_least, least_in,
-    acc_h1, acc_h1t, acc_h0, acc_h0t, acc_x, acc_t, acc_last, acc_o, acc_c1, acc_c0, acc_cx,
+    acc_h1, acc_h1t, acc_h0, acc_h0t, acc_x, acc_t, acc_last, acc_o, acc_c1, acc_c0, acc_cx, actor_rows,
     part_c, part_a, sum_c, sum_a, in_h1, in_h0, in_sm, in_ac,
     fold_s, fold_r, sem_far_s, sem_far_r, sem_param_s, sem_param_r, sem_least_s, sem_least_r, es_s, es_r,
     rs_s, rs_r, ag_s, ag_r, xf_s, xf_r, ef_s, ef_r, sem_out, *boxes,
@@ -306,6 +306,8 @@
         sample = jnp.tanh(latent) * ok8
         return sample, logp, th, spread_e
 
+    actor_rows[...] = jnp.zeros_like(actor_rows)
+
     put_x()
 
     @pl.when(online)
@@ -378,10 +380,11 @@
         fold_in()
         if fold:
             put_x()
-        for what in range(3):
-            param_copy(what).wait_recv()
+        param_copy(0).wait_recv()
         prep_small(small_in.at[0:24], small_in.at[24:32], w1, vec, eq, ga, t1w)
+        param_copy(1).wait_recv()
         half_hidden(0, high_in)
+        param_copy(2).wait_recv()
         half_hidden(1, rest_in)
 
     def least_out():
@@ -539,12 +542,6 @@
             if fold:
                 unit_sum.first_to_core(0, unit_f[0:8, 0:half])
             least_out()
-
-            @pl.when(online)
-            def _():
-                param_copy(3).start()
-                param_copy(4).start()
-
 
         sl = pl.ds(pl.multiple_of(i * block, block), block)
         h, a1, q1 = curves(dot(w1[...], x_b[:, sl]))
@@ -587,6 +584,12 @@
         unit_sum.begin(unit_f[0:8, 0:half], unit_f[0:8, half:rows])
         unit_sum.middle()
 
+    @pl.when(online)
+    def _():
+        for what in (3, 4):
+            param_copy(what).start()
+
+
     class Exchange:
         def __init__(self, index, part, into, inbox, base, count, wide):
             self.index, self.part, self.into, self.inbox, self.base, self.count, self.wide = index, part, into, inbox, base, count, wide
@@ -848,16 +851,14 @@
         lax.fori_loop(0, blocks, body_c, 0)
         part_a[0:HID, :] = acc_c0[0:HID, :]
         part_a[HID : 2 * HID, :] = acc_c1[0:HID, :]
-        stats = jnp.where(lane == 0, actor_sum, jnp.where(lane == 1, count, jnp.where(lane == 2, done_rows, 0.0)))
-        small = acc_cx[...]
-        small = small + jnp.where(rid32 == 18, acc_c0[HID : HID + 1, :], 0.0)
-        small = small + jnp.where(rid32 == 19, acc_c1[HID : HID + 1, :], 0.0)
-        small = small + jnp.where(rid32 == 20, acc_o[16:17, :], 0.0)
-        small = small + jnp.where(rid32 == 21, stats, 0.0)
-        part_a[2 * HID : 2 * HID + 32, :] = small
-        part_a[2 * HID + 32 : 2 * HID + 48, :] = acc_o[0:16, :]
-        rest = part_a.shape[0] - 2 * HID - 48
-        part_a[2 * HID + 48 :, :] = jnp.zeros((rest, HID), F32)
+        actor_rows[0:1, :] = jnp.where(lane == 0, actor_sum, jnp.where(lane == 1, count, jnp.where(lane == 2, done_rows, 0.0)))
+        actor_rows[1:2, :] = acc_o[16:17, :]
+        first = 2 * HID
+        part_a[first : first + 18, :] = acc_cx[0:18, :]
+        part_a[first + 18 : first + 19, :] = acc_c0[HID : HID + 1, :]
+        part_a[first + 19 : first + 20, :] = acc_c1[HID : HID + 1, :]
+        part_a[first + 20 : first + 32, :] = acc_o[0 : 2 * ACT, :]
+        part_a[first + 32 :, :] = jnp.zeros((part_a.shape[0] - first - 32, HID), F32)
         for ex in actor:
             ex.start()
 
@@ -965,13 +966,6 @@
     lax.fori_loop(0, blocks, body_b2, 0)
     part_c[0:HID, :] = acc_h0[0:HID, :] + 0.5 * acc_h0t[...]
     ex_h0.start()
-    ex_h1.reduce()
-
-    @pl.when(targetd)
-    def _():
-        for ex in actor:
-            ex.detour()
-
     lax.fori_loop(0, blocks, body_b3, 0)
     errors, diverse, dv_sum = (jnp.sum(row_sums[k : k + 1, :], axis=1, keepdims=True) for k in range(3))
     stats = jnp.where(lane == 0, errors, jnp.where(lane == 1, diverse, 0.0))
@@ -979,6 +973,7 @@
     small = small + jnp.where(rid32 == 18, acc_h0[HID : HID + 1, :], 0.0)
     small = small + jnp.where(rid32 == 19, acc_h1[HID : HID + 1, :], 0.0)
     small = small + jnp.where(rid32 == 20, stats, 0.0)
+    small = small + jnp.where(rid32 == 21, actor_rows[0:1, :], 0.0) + jnp.where(rid32 == 30, actor_rows[1:2, :], 0.0)
     small = small + jnp.where(rid32 == 22, jnp.where(lane == 0, dv_sum, 0.0), 0.0)
     small = small + jnp.where(rid32 == 23, acc_last[0:1, :], 0.0)
     part_c[2 * HID : 2 * HID + 24, :] = small[0:24]
@@ -987,9 +982,16 @@
     if rest:
         part_c[2 * HID + 32 :, :] = jnp.zeros((rest, HID), F32)
     ex_sm.start()
-    ex_h1.forward()
+
+    @pl.when(targetd)
+    def _():
+        for ex in actor:
+            ex.detour()
+
+    ex_h1.reduce()
     ex_h0.reduce()
     ex_sm.reduce()
+    ex_h1.forward()
 
     @pl.when(targetd)
     def _():
@@ -1019,21 +1021,27 @@
         for copy in far_outputs():
             copy.start()
 
+    def out_rows(first, last, k):
+        return local(sum_c.at[:, first:last], out_c.at[:, first:last], k)
+
+    copies = [out_rows(HID, 2 * HID, 4), local(sum_a, out_a, 3), out_rows(2 * HID, sum_c.shape[1], 6), out_rows(0, HID, 7)]
+    ex_h1.arrived()
+    if coded:
+        ex_h1.decode()
+    copies[0].start()
     for k in range(1, 4):
         spread_actor(k).wait_recv()
         if coded:
             spread_scale(k).wait_recv()
     if coded:
         ex_ac.decode()
-    copy_a = local(sum_a, out_a, 3)
-    copy_a.start()
-    for ex in (ex_h1, ex_h0, ex_sm):
-        ex.arrived()
+    copies[1].start()
+    ex_sm.arrived()
+    copies[2].start()
+    ex_h0.arrived()
     if coded:
-        ex_h1.decode()
         ex_h0.decode()
-    copy_c = local(sum_c, out_c, 4)
-    copy_c.start()
+    copies[3].start()
 
     @pl.when(online)
     def _():
@@ -1076,8 +1084,8 @@
             spread_scale(k).wait_send()
     for ex in (ex_h1, ex_h0, ex_sm):
         ex.sent()
-    copy_a.wait()
-    copy_c.wait()
+    for copy in copies:
+        copy.wait()
 
     @pl.when(online)
     def _():
@@ -1126,14 +1134,14 @@
         v((1, size), F32), v((1, 2 * extra), F32), v((4, 1, rows), F32),
         v((272, HID), F32), v((HID, HID), F32), v((272, HID), F32), v((HID, HID), F32),
         v((32, HID), F32), v((16, HID), F32), v((8, HID), F32), v((32, HID), F32),
-        v((272, HID), F32), v((272, HID), F32), v((32, HID), F32),
+        v((272, HID), F32), v((272, HID), F32), v((32, HID), F32), v((8, HID), F32),
         v((size_c, HID), F32), v((size_a, HID), F32), v((2, size_c, HID), F32), v((size_a, HID), F32),
         *[v((1, 8, HID) if coded else (n_dp - 1, HID // n_dp, HID), F32) for _ in range(2)],
         v((n_dp - 1, (size_c - 2 * HID) // n_dp, HID), F32),
         v((n_dp - 1, (ACTOR_SMALL if coded else size_a // 4) // n_dp, HID), F32),
         dma((2, 2)), dma((2, 2)), dma, dma, dma((5,)), dma((5,)), dma((8,)), dma((4,)), dma((2, 5)), dma((2, 5)),
         dma((5, n_dp - 1, 2)), dma((5, n_dp - 1, 2)), dma((5, n_dp - 1, 2)), dma((5, n_dp - 1, 2)), dma((5, n_dp, 2)), dma((5, n_dp, 2)),
-        dma((6,)), dma((6,)), dma((6,)),
+        dma((6,)), dma((6,)), dma((8,)),
     ]
     if coded:
         for each, lead in ((HID // n_dp, 2), (HID // n_dp, 2), (2 * HID // (4 * n_dp), 4)):
@@ -1159,7 +1167,11 @@
 def adamw(param, grad, first, second):
     first_new = BETA_ONE * first + (1.0 - BETA_ONE) * grad
     second_new = BETA_TWO * second + (1.0 - BETA_TWO) * grad * grad
-    ratio = first_new / (1.0 - BETA_ONE**STEP) / (jnp.sqrt(second_new / (1.0 - BETA_TWO**STEP)) + EPS)
+    scaled = second_new * (1.0 / (1.0 - BETA_TWO**STEP))
+    root = scaled * lax.rsqrt(jnp.maximum(scaled, 1e-30)) + EPS
+    inverse = pl.reciprocal(root, approx=True)
+    inverse = inverse * (2.0 - root * inverse)
+    ratio = first_new * (1.0 / (1.0 - BETA_ONE**STEP)) * inverse
     return (param - LEARN * (ratio + DECAY * param), first_new, second_new)
 
 
@@ -1195,8 +1207,8 @@
         rows = slice(k * HID, (k + 1) * HID)
         return [read(ga, k, lambda r: r.at[rows])] + [read(b, k, lambda r: r.at[k]) for b in (ah, ahm, ahv)]
 
-    stats = read(ga, 2, lambda r: r.at[2 * HID : 2 * HID + ACTOR_SMALL])
-    small_reads = [read(gc, 4, lambda r: r.at[:, 2 * HID :]), stats] + [
+    stats = read(gc, 4, lambda r: r.at[:, 2 * HID :])
+    small_reads = [read(ga, 2, lambda r: r.at[2 * HID : 2 * HID + ACTOR_SMALL]), stats] + [
         read(b) for b in (own_e, own_b, on_s, em, ev, bm, bv, ae, ab, aem, aev, abm, abv)
     ]
     order = [(0, 0), (0, 1), (1, 0), (1, 1)]
@@ -1215,7 +1227,8 @@
 
     gas = ga.at[2 * HID : 2 * HID + ACTOR_SMALL]
     stats.wait()
-    scale = 1.0 / gas[21:22, 1:2]
+    rows_a = gc.at[1, 2 * HID : 2 * HID + 32]
+    scale = 1.0 / rows_a[21:22, 1:2]
     writes = []
 
     def put(copy):
@@ -1252,12 +1265,12 @@
         o_b[m], o_bm[m], o_bv[m] = critic(own_b[m], on_s[first + 24 : first + 28], gb[...] * scale, bm[m], bv[m])
         o_ms[m : m + 1, :] = small[20:21, 0:2]
     gae[0:OBS, :] = gas[0:OBS, :]
-    gae[OBS : OBS + 2 * ACT, :] = gas[32 : 32 + 2 * ACT, :]
+    gae[OBS : OBS + 2 * ACT, :] = gas[20 : 20 + 2 * ACT, :]
     gab[0:3, :] = gas[17:20, :]
-    gab[3:4, :] = gas[20:21, :]
+    gab[3:4, :] = rows_a[30:31, :]
     o_ae[...], o_aem[...], o_aev[...] = adamw(ae[...], gae[...] * scale, aem[...], aev[...])
     o_ab[...], o_abm[...], o_abv[...] = adamw(ab[...], gab[...] * scale, abm[...], abv[...])
-    o_as[...] = gas[21:22, 0:2]
+    o_as[...] = rows_a[21:22, 0:2]
     for r in (o_e, o_b, o_em, o_ev, o_bm, o_bv, o_ae, o_ab, o_aem, o_aev, o_abm, o_abv, o_ms, o_as):
         put(write(r))
     for at in order[1:]:
@@ -1323,7 +1336,7 @@
         more_c, more_a, *_ = fused(n_dp, size, size // 16, False, (*data, left.astype(F32)[None]), own, aparams)
         return finish(grad_c + more_c, grad_a + more_a)
 
-    sums = grad_a[2 * HID + 21]
+    sums = grad_c[1, 2 * HID + 21]
     out = lax.cond(sums[1] != sums[2], with_rest, lambda: finish(grad_c, grad_a))
     return (*(o[None] for o in out[:3]), *out[3:19], out[19][0])
 

time: 74.1 us -> 72.5 us (0.978)
  Pallas kernels: 69.4 us -> 67.1 us
    pallas_call x1, Pallas kernels: 62.7 us -> 60.2 us  [fused(): pl.pallas_call(functools.partial(kernel, n_dp, rows, block, fold), out_sh...]
where the time goes in v2:
time: 72.5 us; the launch traced here: 71.6 us
  Pallas kernels  67.1 us (93%)
  between operations  2.89 us (4%)
  local copies, waits for them, and re-layouts  1.36 us (2%)
    pallas_call x1, Pallas kernels, fused(): pl.pallas_call(functools.partial(kernel, n_dp, rows, block, fold), out_sh...  60.2 us
    pallas_call x1, Pallas kernels, update(): pl.pallas_call(update_kernel, out_shape=outs, in_specs=[anyspace] * len(a...  6.88 us

profile of v2, /device:TPU:0, one launch (start us, length us, event | category | flops | bytes accessed | tf_op | source)
XLA Modules:
  0.0 71.6 jit_solution(7340853089792459297)
XLA Ops:
  1.3 0.0 copy-start.1
  1.3 0.0 copy-start.7
  1.3 0.0 copy-start.9
  1.3 0.0 copy-start.12
  1.3 0.0 copy-start.18
  1.4 0.0 copy-start.19
  1.4 60.2 %edac_gradients.1 = (f32[2,544,256]{2,1,0:T(8,128)}, f32[640,256]{1,0:T(8,128)}, f32[64,256]{1,0:T(8,128)S(1)}, bf16[512,256]{1,0:T(8,128)(2,1)}, bf16[512,256]{1,0:T(8,128)(2,1)}, /*index=5*/bf16[512,256]{1,0:T(8,128)(2,1)}) custom-call(f32[34,4096]{1,0:T(8,128)} %bitcast.22, f32[6,4096]{1,0:T(8,128)} %bitcast.29, f32[12,4096]{1,0:T(8,128)} %bitcast.24, ...), custom_call_target="tpu_custom_call" | custom-call | tf_op jit(solution)/shard_map/edac_gradients/pallas_call | solution.py:1154
  61.6 1.3 %fusion = (f32[1,1,1]{2,1,0:T(1,128)}, f32[1,1,1]{2,1,0:T(1,128)}) fusion(f32[2,544,256]{2,1,0:T(8,128)} %get-tuple-element.294), kind=kLoop, calls=%fused_computation.5 | loop fusion | bytes 16 | tf_op jit(solution)/shard_map/slice | solution.py:1340
  64.2 0.0 copy-done.1
  64.3 0.0 copy-done.7
  64.3 0.0 copy-done.9
  64.3 0.0 copy-done.12
  64.3 0.0 copy-done.18
  64.3 0.0 copy-done.19
  64.3 7.1 %conditional.1 = (f32[2,24,256]{2,1,0:T(8,128)}, f32[2,24,256]{2,1,0:T(8,128)}, f32[2,2,256,256]{3,2,1,0:T(8,128)}, f32[2,2,256,256]{3,2,1,0:T(8,128)}, f32[2,4,...) conditional(s32[]{:T(128)} %bitcast.18, ...), branch_computations={%region_0.0_spmd, %region_1.2_spmd} | conditional | flops 548885 | bytes 27362168 | solution.py:1340
  64.5 6.9 %adamw.2 = (f32[2,24,256]{2,1,0:T(8,128)}, f32[2,2,256,256]{3,2,1,0:T(8,128)}, f32[2,4,256]{2,1,0:T(4,128)}, f32[2,24,256]{2,1,0:T(8,128)}, f32[2,24,256]{2,1,0:...) custom-call(f32[2,544,256]{2,1,0:T(8,128)} %get-tuple-element.152.re, ...), custom_call_target="tpu_custom_call" | custom-call | tf_op jit(solution)/shard_map/cond/branch_0_fun/adamw/pallas_call | solution.py:1297
Async XLA Ops:
  1.3 62.9 %copy-start.1 = (f32[2,256,256]{2,1,0:T(8,128)S(1)}, f32[2,256,256]{2,1,0:T(8,128)}, u32[]{:S(2)}) copy-start(f32[2,256,256]{2,1,0:T(8,128)} %a_hidden.1) | copy-start | bytes 1572868
  1.3 62.9 %copy-start.7 = (f32[4096,12]{0,1:T(8,128)S(1)}, f32[4096,12]{0,1:T(8,128)}, u32[]{:S(2)}) copy-start(f32[4096,12]{0,1:T(8,128)} %param.30) | copy-start | bytes 589828
  1.3 62.9 %copy-start.9 = (f32[1,2,24,256]{3,2,1,0:T(8,128)S(1)}, f32[1,2,24,256]{3,2,1,0:T(8,128)}, u32[]{:S(2)}) copy-start(f32[1,2,24,256]{3,2,1,0:T(8,128)} %param.32) | copy-start | bytes 147460
  1.3 62.9 %copy-start.12 = (f32[29,256]{1,0:T(8,128)S(1)}, f32[29,256]{1,0:T(8,128)}, u32[]{:S(2)}) copy-start(f32[29,256]{1,0:T(8,128)} %a_edge.1) | copy-start | bytes 89092
  1.3 62.9 %copy-start.18 = (f32[4096]{0:T(1024)S(1)}, f32[4096]{0:T(1024)}, u32[]{:S(2)}) copy-start(f32[4096]{0:T(1024)} %param.28) | copy-start | bytes 49156
  1.4 62.9 %copy-start.19 = (f32[29,256]{1,0:T(8,128)S(1)}, f32[29,256]{1,0:T(8,128)}, u32[]{:S(2)}) copy-start(f32[29,256]{1,0:T(8,128)} %param.44) | copy-start | bytes 89092

commit v3 on v2

--- a/solution.py
+++ b/solution.py
@@ -1262,14 +1262,16 @@
         gb[3:4, :] = small[22:23, :]
         first = 32 * (1 - m)
         o_e[m], o_em[m], o_ev[m] = critic(own_e[m], on_s[first : first + 24], ge[...] * scale, em[m], ev[m])
-        o_b[m], o_bm[m], o_bv[m] = critic(own_b[m], on_s[first + 24 : first + 28], gb[...] * scale, bm[m], bv[m])
-        o_ms[m : m + 1, :] = small[20:21, 0:2]
+        o_b[m], o_bm[m], o_bv[m] = critic(own_b[m], on_s[first + 24 : first + 28], gb[0:4, :] * scale, bm[m], bv[m])
+    second = lax.broadcasted_iota(jnp.int32, (2, 2), 0) == 1
+    row = 2 * HID + 20
+    o_ms[...] = jnp.where(second, gc[0, row : row + 1, 0:2], gc[1, row : row + 1, 0:2])
     gae[0:OBS, :] = gas[0:OBS, :]
     gae[OBS : OBS + 2 * ACT, :] = gas[20 : 20 + 2 * ACT, :]
     gab[0:3, :] = gas[17:20, :]
     gab[3:4, :] = rows_a[30:31, :]
-    o_ae[...], o_aem[...], o_aev[...] = adamw(ae[...], gae[...] * scale, aem[...], aev[...])
-    o_ab[...], o_abm[...], o_abv[...] = adamw(ab[...], gab[...] * scale, abm[...], abv[...])
+    o_ae[...], o_aem[...], o_aev[...] = adamw(ae[...], gae[0:29, :] * scale, aem[...], aev[...])
+    o_ab[...], o_abm[...], o_abv[...] = adamw(ab[...], gab[0:4, :] * scale, abm[...], abv[...])
     o_as[...] = rows_a[21:22, 0:2]
     for r in (o_e, o_b, o_em, o_ev, o_bm, o_bv, o_ae, o_ab, o_aem, o_aev, o_abm, o_abv, o_ms, o_as):
         put(write(r))
@@ -1301,7 +1303,7 @@
         out_specs=(anyspace,) * len(outs),
         scratch_shapes=room
         + [pltpu.VMEM(o.shape, o.dtype) for o in outs]
-        + [pltpu.VMEM((24, HID), F32), pltpu.VMEM((4, HID), F32), pltpu.VMEM((29, HID), F32), pltpu.VMEM((4, HID), F32)]
+        + [pltpu.VMEM((24, HID), F32), pltpu.VMEM((8, HID), F32), pltpu.VMEM((32, HID), F32), pltpu.VMEM((8, HID), F32)]
         + [pltpu.SemaphoreType.DMA((len(args), 5)), pltpu.SemaphoreType.DMA((len(outs), 4))],
         compiler_params=pltpu.CompilerParams(vmem_limit_bytes=40 * 2**20),
         name="adamw",

time: 72.5 us -> 72.5 us (level)
  no operation moved by 1% of the time
where the time goes in v3:
time: 72.5 us; the launch traced here: 71.6 us
  Pallas kernels  67.1 us (93%)
  between operations  2.89 us (4%)
  local copies, waits for them, and re-layouts  1.36 us (2%)
    pallas_call x1, Pallas kernels, fused(): pl.pallas_call(functools.partial(kernel, n_dp, rows, block, fold), out_sh...  60.2 us
    pallas_call x1, Pallas kernels, update(): pl.pallas_call(update_kernel, out_shape=outs, in_specs=[anyspace] * len(a...  6.88 us

profile of v3, /device:TPU:0, one launch (start us, length us, event | category | flops | bytes accessed | tf_op | source)
XLA Modules:
  0.0 71.6 jit_solution(3719870316404978151)
XLA Ops:
  1.3 0.0 copy-start.1
  1.3 0.0 copy-start.7
  1.3 0.0 copy-start.9
  1.3 0.0 copy-start.12
  1.3 0.0 copy-start.18
  1.4 0.0 copy-start.19
  1.4 60.2 %edac_gradients.1 = (f32[2,544,256]{2,1,0:T(8,128)}, f32[640,256]{1,0:T(8,128)}, f32[64,256]{1,0:T(8,128)S(1)}, bf16[512,256]{1,0:T(8,128)(2,1)}, bf16[512,256]{1,0:T(8,128)(2,1)}, /*index=5*/bf16[512,256]{1,0:T(8,128)(2,1)}) custom-call(f32[34,4096]{1,0:T(8,128)} %bitcast.22, f32[6,4096]{1,0:T(8,128)} %bitcast.29, f32[12,4096]{1,0:T(8,128)} %bitcast.24, ...), custom_call_target="tpu_custom_call" | custom-call | tf_op jit(solution)/shard_map/edac_gradients/pallas_call | solution.py:1154
  61.6 1.3 %fusion = (f32[1,1,1]{2,1,0:T(1,128)}, f32[1,1,1]{2,1,0:T(1,128)}) fusion(f32[2,544,256]{2,1,0:T(8,128)} %get-tuple-element.294), kind=kLoop, calls=%fused_computation.5 | loop fusion | bytes 16 | tf_op jit(solution)/shard_map/slice | solution.py:1342
  64.2 0.0 copy-done.1
  64.3 0.0 copy-done.7
  64.3 0.0 copy-done.9
  64.3 0.0 copy-done.12
  64.3 0.0 copy-done.18
  64.3 0.0 copy-done.19
  64.3 7.1 %conditional.1 = (f32[2,24,256]{2,1,0:T(8,128)}, f32[2,24,256]{2,1,0:T(8,128)}, f32[2,2,256,256]{3,2,1,0:T(8,128)}, f32[2,2,256,256]{3,2,1,0:T(8,128)}, f32[2,4,...) conditional(s32[]{:T(128)} %bitcast.18, ...), branch_computations={%region_0.0_spmd, %region_1.2_spmd} | conditional | flops 548885 | bytes 27362168 | solution.py:1342
  64.5 6.9 %adamw.2 = (f32[2,24,256]{2,1,0:T(8,128)}, f32[2,2,256,256]{3,2,1,0:T(8,128)}, f32[2,4,256]{2,1,0:T(4,128)}, f32[2,24,256]{2,1,0:T(8,128)}, f32[2,24,256]{2,1,0:...) custom-call(f32[2,544,256]{2,1,0:T(8,128)} %get-tuple-element.152.re, ...), custom_call_target="tpu_custom_call" | custom-call | tf_op jit(solution)/shard_map/cond/branch_0_fun/adamw/pallas_call | solution.py:1299
Async XLA Ops:
  1.3 62.9 %copy-start.1 = (f32[2,256,256]{2,1,0:T(8,128)S(1)}, f32[2,256,256]{2,1,0:T(8,128)}, u32[]{:S(2)}) copy-start(f32[2,256,256]{2,1,0:T(8,128)} %a_hidden.1) | copy-start | bytes 1572868
  1.3 62.9 %copy-start.7 = (f32[4096,12]{0,1:T(8,128)S(1)}, f32[4096,12]{0,1:T(8,128)}, u32[]{:S(2)}) copy-start(f32[4096,12]{0,1:T(8,128)} %param.30) | copy-start | bytes 589828
  1.3 62.9 %copy-start.9 = (f32[1,2,24,256]{3,2,1,0:T(8,128)S(1)}, f32[1,2,24,256]{3,2,1,0:T(8,128)}, u32[]{:S(2)}) copy-start(f32[1,2,24,256]{3,2,1,0:T(8,128)} %param.32) | copy-start | bytes 147460
  1.3 62.9 %copy-start.12 = (f32[29,256]{1,0:T(8,128)S(1)}, f32[29,256]{1,0:T(8,128)}, u32[]{:S(2)}) copy-start(f32[29,256]{1,0:T(8,128)} %a_edge.1) | copy-start | bytes 89092
  1.3 62.9 %copy-start.18 = (f32[4096]{0:T(1024)S(1)}, f32[4096]{0:T(1024)}, u32[]{:S(2)}) copy-start(f32[4096]{0:T(1024)} %param.28) | copy-start | bytes 49156
  1.4 62.9 %copy-start.19 = (f32[29,256]{1,0:T(8,128)S(1)}, f32[29,256]{1,0:T(8,128)}, u32[]{:S(2)}) copy-start(f32[29,256]{1,0:T(8,128)} %param.44) | copy-start | bytes 89092

commit v4 on v3

--- a/solution.py
+++ b/solution.py
@@ -991,7 +991,6 @@
     ex_h1.reduce()
     ex_h0.reduce()
     ex_sm.reduce()
-    ex_h1.forward()
 
     @pl.when(targetd)
     def _():
@@ -999,14 +998,16 @@
             ex.forward()
         spread_start()
 
-    ex_h0.forward()
-    ex_sm.forward()
-
     @pl.when(online)
     def _():
         for ex in actor:
             ex.back()
         spread_start()
+
+    ex_h1.forward()
+
+    ex_h0.forward()
+    ex_sm.forward()
 
 
     @pl.when(online)

time: 72.5 us -> 71.9 us (level)
  no operation moved by 1% of the time
where the time goes in v4:
time: 71.9 us; the launch traced here: 71.6 us
  Pallas kernels  67.1 us (93%)
  between operations  2.89 us (4%)
  local copies, waits for them, and re-layouts  1.36 us (2%)
    pallas_call x1, Pallas kernels, fused(): pl.pallas_call(functools.partial(kernel, n_dp, rows, block, fold), out_sh...  60.2 us
    pallas_call x1, Pallas kernels, update(): pl.pallas_call(update_kernel, out_shape=outs, in_specs=[anyspace] * len(a...  6.88 us

profile of v4, /device:TPU:0, one launch (start us, length us, event | category | flops | bytes accessed | tf_op | source)
XLA Modules:
  0.0 71.6 jit_solution(17349264687478557212)
XLA Ops:
  1.3 0.0 copy-start.1
  1.3 0.0 copy-start.7
  1.3 0.0 copy-start.9
  1.3 0.0 copy-start.12
  1.3 0.0 copy-start.18
  1.4 0.0 copy-start.19
  1.4 60.2 %edac_gradients.1 = (f32[2,544,256]{2,1,0:T(8,128)}, f32[640,256]{1,0:T(8,128)}, f32[64,256]{1,0:T(8,128)S(1)}, bf16[512,256]{1,0:T(8,128)(2,1)}, bf16[512,256]{1,0:T(8,128)(2,1)}, /*index=5*/bf16[512,256]{1,0:T(8,128)(2,1)}) custom-call(f32[34,4096]{1,0:T(8,128)} %bitcast.22, f32[6,4096]{1,0:T(8,128)} %bitcast.29, f32[12,4096]{1,0:T(8,128)} %bitcast.24, ...), custom_call_target="tpu_custom_call" | custom-call | tf_op jit(solution)/shard_map/edac_gradients/pallas_call | solution.py:1155
  61.6 1.3 %fusion = (f32[1,1,1]{2,1,0:T(1,128)}, f32[1,1,1]{2,1,0:T(1,128)}) fusion(f32[2,544,256]{2,1,0:T(8,128)} %get-tuple-element.294), kind=kLoop, calls=%fused_computation.5 | loop fusion | bytes 16 | tf_op jit(solution)/shard_map/slice | solution.py:1343
  64.2 0.0 copy-done.1
  64.3 0.0 copy-done.7
  64.3 0.0 copy-done.9
  64.3 0.0 copy-done.12
  64.3 0.0 copy-done.18
  64.3 0.0 copy-done.19
  64.3 7.1 %conditional.1 = (f32[2,24,256]{2,1,0:T(8,128)}, f32[2,24,256]{2,1,0:T(8,128)}, f32[2,2,256,256]{3,2,1,0:T(8,128)}, f32[2,2,256,256]{3,2,1,0:T(8,128)}, f32[2,4,...) conditional(s32[]{:T(128)} %bitcast.18, ...), branch_computations={%region_0.0_spmd, %region_1.2_spmd} | conditional | flops 548885 | bytes 27362168 | solution.py:1343
  64.5 6.9 %adamw.2 = (f32[2,24,256]{2,1,0:T(8,128)}, f32[2,2,256,256]{3,2,1,0:T(8,128)}, f32[2,4,256]{2,1,0:T(4,128)}, f32[2,24,256]{2,1,0:T(8,128)}, f32[2,24,256]{2,1,0:...) custom-call(f32[2,544,256]{2,1,0:T(8,128)} %get-tuple-element.152.re, ...), custom_call_target="tpu_custom_call" | custom-call | tf_op jit(solution)/shard_map/cond/branch_0_fun/adamw/pallas_call | solution.py:1300
Async XLA Ops:
  1.3 62.9 %copy-start.1 = (f32[2,256,256]{2,1,0:T(8,128)S(1)}, f32[2,256,256]{2,1,0:T(8,128)}, u32[]{:S(2)}) copy-start(f32[2,256,256]{2,1,0:T(8,128)} %a_hidden.1) | copy-start | bytes 1572868
  1.3 62.9 %copy-start.7 = (f32[4096,12]{0,1:T(8,128)S(1)}, f32[4096,12]{0,1:T(8,128)}, u32[]{:S(2)}) copy-start(f32[4096,12]{0,1:T(8,128)} %param.30) | copy-start | bytes 589828
  1.3 62.9 %copy-start.9 = (f32[1,2,24,256]{3,2,1,0:T(8,128)S(1)}, f32[1,2,24,256]{3,2,1,0:T(8,128)}, u32[]{:S(2)}) copy-start(f32[1,2,24,256]{3,2,1,0:T(8,128)} %param.32) | copy-start | bytes 147460
  1.3 62.9 %copy-start.12 = (f32[29,256]{1,0:T(8,128)S(1)}, f32[29,256]{1,0:T(8,128)}, u32[]{:S(2)}) copy-start(f32[29,256]{1,0:T(8,128)} %a_edge.1) | copy-start | bytes 89092
  1.3 62.9 %copy-start.18 = (f32[4096]{0:T(1024)S(1)}, f32[4096]{0:T(1024)}, u32[]{:S(2)}) copy-start(f32[4096]{0:T(1024)} %param.28) | copy-start | bytes 49156
  1.4 62.9 %copy-start.19 = (f32[29,256]{1,0:T(8,128)S(1)}, f32[29,256]{1,0:T(8,128)}, u32[]{:S(2)}) copy-start(f32[29,256]{1,0:T(8,128)} %param.44) | copy-start | bytes 89092
